TPU v7x, 256 devices: a whole 4x4x8 slice. The times are simulated.
256 devices in a mesh: gx: 16 (over z, core), gy: 4 (over x), gz: 4 (over y).
Axes of the slice: x: 4, y: 4, z: 8, core: 2. Of those that a mesh axis runs over, the one named last changes fastest.
Arguments:
- density: float32 [512, 128, 512], P('gx', 'gy', 'gz'), may hold values from 0.8 to 1.25
- momentum: float32 [3, 512, 128, 512], P(None, 'gx', 'gy', 'gz'), may hold values from -1 to 1
- energy: float32 [512, 128, 512], P('gx', 'gy', 'gz'), may hold values from 3 to 4
- metric: float32 [128], replicated, may hold values from 0.5 to 4
Outputs:
- tendency: float32 [5, 512, 128, 512], P(None, 'gx', 'gy', 'gz')
- state_next: float32 [5, 512, 128, 512], P(None, 'gx', 'gy', 'gz')
All inputs are finite; a program needn't handle non-finite values.
Results may differ from a plain program's by a relative error of at most 0.0003.
Values sent between devices are 32-bit elements; how exact they have to be, the bound alone decides.
A program may use at most 128 MiB of HBM per device.

v0:
```python
import functools

import jax
import jax.numpy as jnp
import numpy as np
from jax import lax
from jax.experimental import pallas as pl
from jax.experimental.pallas import tpu as pltpu
from jax.sharding import PartitionSpec as P

heat_ratio = 1.4
compact_alpha = 1.0 / 3.0
filter_alpha = 0.499
time_step = 0.05
near_weight = 7.0 / 9.0
wide_weight = 1.0 / 36.0
HIGH = lax.Precision.HIGHEST
MESH = pl.DeviceIdType.MESH
KINDS_Y = ((1, "last"), (1, "ml"), (1, "mr"), (2, "ml"), (2, "mr"), (3, "ml"), (3, "mr"), (3, "first"))


def decay(alpha):
    root = np.sqrt(1.0 - 4.0 * alpha * alpha)
    return (-1.0 + root) / (2.0 * alpha), 1.0 / root


def compact_kernel():
    ratio, gain = decay(compact_alpha)

    def green(n):
        return gain * ratio ** abs(n)

    def kernel(d):
        return near_weight * (green(d + 1) - green(d - 1)) + wide_weight * (green(d + 2) - green(d - 2))

    amplitude = kernel(2) / ratio**2
    return ratio, amplitude, kernel(1) - amplitude * ratio


def local_compact(size):
    ratio, amplitude, corner = compact_kernel()
    table = np.zeros((size, size))
    for i in range(size):
        for j in range(size):
            d = abs(i - j)
            if d:
                value = amplitude * ratio**d + (corner if d == 1 else 0.0)
                table[i, j] = value if i > j else -value
    return table


def table_thomas(lower_band, main_band, upper_band, source):
    count = source.shape[0]
    c_all = np.zeros(count)
    d_all = np.zeros(source.shape)
    c_prev = 0.0
    d_prev = np.zeros(source.shape[1:])
    for place in range(count):
        denom = main_band[place] - lower_band[place] * c_prev
        c_prev = upper_band[place] / denom
        d_prev = (source[place] - lower_band[place] * d_prev) / denom
        c_all[place] = c_prev
        d_all[place] = d_prev
    solved = np.zeros(source.shape)
    x_next = np.zeros(source.shape[1:])
    for place in range(count - 1, -1, -1):
        x_next = d_all[place] - c_all[place] * x_next
        solved[place] = x_next
    return solved


def wall_bands(total):
    lower = np.full(total, compact_alpha)
    upper = np.full(total, compact_alpha)
    lower[0], lower[1], lower[total - 2], lower[total - 1] = 0.0, 0.25, 0.25, 2.0
    upper[0], upper[1], upper[total - 2], upper[total - 1] = 2.0, 0.25, 0.25, 0.0
    return lower, upper


def wall_table(total):
    lower, upper = wall_bands(total)
    stencil = np.zeros((total, total))
    for i in range(2, total - 2):
        stencil[i, i + 1], stencil[i, i - 1] = near_weight, -near_weight
        stencil[i, i + 2], stencil[i, i - 2] = wide_weight, -wide_weight
    for i in (1, total - 2):
        stencil[i, i + 1], stencil[i, i - 1] = 0.75, -0.75
    stencil[0, :3] = (-2.5, 2.0, 0.5)
    stencil[total - 1, total - 3 :] = (-0.5, -2.0, 2.5)
    return table_thomas(lower, np.ones(total), upper, stencil)


@functools.cache
def wall_tables(blocks, size):
    total = blocks * size
    table = wall_table(total)
    lower, upper = wall_bands(total)
    down = np.zeros(total)
    for i in range(total - 1, 0, -1):
        down[i - 1] = -lower[i] / (1.0 + upper[i] * down[i])
    up = np.zeros(total)
    for i in range(total - 1):
        up[i + 1] = -upper[i] / (1.0 + lower[i] * up[i])
    carry_l, carry_r, corner_l, corner_r = [], [], [], []
    moment_l, moment_r = np.zeros((blocks, size)), np.zeros((blocks, size))
    for b in range(blocks):
        head, tail = b * size, b * size + size - 1
        carry_l.append(np.concatenate([[1.0], np.cumprod(down[head:tail])]))
        carry_r.append(np.concatenate([[1.0], np.cumprod(up[head + 1 : tail + 1][::-1])])[::-1])
        corner_l.append(table[head, head - 1] - table[head + 1, head - 1] / down[head] if b else 0.0)
        corner_r.append(table[tail, tail + 1] - table[tail - 1, tail + 1] / up[tail] if b < blocks - 1 else 0.0)
        if b < blocks - 1:
            to = tail + 1
            moment_l[b] = table[to, head:to]
            moment_l[b, size - 1] = table[to + 1, tail] / down[to]
        if b:
            to = head - 1
            moment_r[b] = table[to, head : tail + 1]
            moment_r[b, 0] = table[to - 1, head] / up[to]
    apply = np.zeros((blocks, 8 * size + 32, 8 * size))
    carry = np.zeros((blocks, 8 * size, 8 * len(KINDS_Y)))
    eye = np.eye(8)
    for b in range(blocks):
        rows = slice(b * size, (b + 1) * size)
        apply[b, : 8 * size] = np.kron(eye, table[rows, rows])
        first, last = np.eye(size)[0], np.eye(size)[size - 1]
        for kind, weights in enumerate((last, moment_l[b], moment_r[b], first)):
            apply[b, 8 * size + 8 * kind : 8 * size + 8 * kind + 8] = np.kron(eye, weights[None])
        for place, (offset, kind) in enumerate(KINDS_Y):
            column = np.zeros(size)
            if b - offset >= 0:
                if kind == "ml":
                    scale = 1.0
                    for c in range(b - offset + 1, b):
                        scale *= np.prod(down[c * size : (c + 1) * size])
                    column = scale * carry_l[b]
                elif kind == "last" and offset == 1:
                    column[0] = corner_l[b]
            else:
                distance = blocks - offset
                if kind == "mr":
                    scale = 1.0
                    for c in range(b + 1, b + distance):
                        scale *= np.prod(up[c * size : (c + 1) * size])
                    column = scale * carry_r[b]
                elif kind == "first" and distance == 1:
                    column[size - 1] = corner_r[b]
            carry[b, :, 8 * place : 8 * place + 8] = np.kron(eye, column[:, None])
    return apply.astype(np.float32), carry.astype(np.float32)


@functools.cache
def span_tables(blocks, size):
    ratio, amplitude, corner = compact_kernel()
    places = np.arange(size)
    images = 1.0 / (1.0 - ratio ** (blocks * size))
    moments = np.zeros((4, size))
    moments[0, size - 1] = 1.0
    moments[1] = ratio ** (size - places)
    moments[2] = ratio ** (places + 1.0)
    moments[3, 0] = 1.0
    carries = np.zeros((blocks, 4, size))
    for slot in range(blocks):
        behind = slot if slot else blocks
        ahead = blocks - slot
        carries[slot, 1] = amplitude * images * ratio ** (size * (behind - 1.0)) * ratio**places
        carries[slot, 2] = -amplitude * images * ratio ** (size * (ahead - 1.0)) * ratio ** (size - 1.0 - places)
        if behind == 1:
            carries[slot, 0, 0] = corner
        if ahead == 1:
            carries[slot, 3, size - 1] = -corner
    both_moments = np.zeros((8, 2 * size))
    both_moments[:4, :size] = moments
    both_moments[4:, size:] = moments
    both_carries = np.zeros((blocks, 8, 2 * size))
    both_carries[:, :4, :size] = carries
    both_carries[:, 4:, size:] = carries
    return (
        local_compact(size).T.astype(np.float32),
        both_moments.astype(np.float32),
        both_carries.reshape(8 * blocks, 2 * size).astype(np.float32),
    )


def stream_weights(size):
    ratio, amplitude, _ = compact_kernel()
    filter_ratio, _ = decay(filter_alpha)
    places = np.arange(size)
    weight_u = filter_ratio ** (size - places)
    weight_v = filter_ratio ** (places + 1.0)
    local = local_compact(size)
    return np.stack(
        [
            weight_u,
            weight_v,
            -time_step * (weight_u @ local),
            -time_step * (weight_v @ local),
            ratio ** (size - places),
            ratio ** (places + 1.0),
            amplitude * ratio**places,
            amplitude * ratio ** (size - 1.0 - places),
        ]
    )


def exchange_kernel(
    nx,
    ny,
    nz,
    den,
    mom,
    ene,
    metric,
    wtab,
    ky_hbm,
    py_hbm,
    kz,
    qz,
    pz,
    tend,
    carry_x,
    carry_f,
    fx,
    fy,
    fz,
    ky,
    py,
    uv0,
    sy,
    sz,
    dys,
    dzs,
    ys_out,
    ys_in,
    zs_in,
    yb_out,
    yb_in,
    zm_in,
    xn_out,
    xn_in,
    xm_out,
    xm_in,
    uv_out,
    uv_in,
    xo_out,
    xo_in,
    io_out,
    io_in,
    load_sem,
    send_sem,
    recv_sem,
):
    fields, size_x, size_y, size_z = fx.shape
    me_x, me_y, me_z = lax.axis_index("gx"), lax.axis_index("gy"), lax.axis_index("gz")
    rows = size_y // nx
    ratio, amplitude, corner = compact_kernel()
    weights = stream_weights(size_x)
    filter_ratio, _ = decay(filter_alpha)

    def along(axis, offset):
        me, count = {"gx": (me_x, nx), "gy": (me_y, ny), "gz": (me_z, nz)}[axis]
        return lax.rem(me + offset + count, count)

    barrier = pltpu.get_barrier_semaphore()
    for axis, count in (("gx", nx), ("gy", ny), ("gz", nz)):
        for offset in range(1, count):
            pl.semaphore_signal(barrier, inc=1, device_id={axis: along(axis, offset)}, device_id_type=MESH)

    loads = [
        pltpu.make_async_copy(ky_hbm.at[me_y], ky, load_sem.at[0]),
        pltpu.make_async_copy(py_hbm.at[me_y], py, load_sem.at[1]),
    ]
    for load in loads:
        load.start()

    next_sem = [0]

    def remote(src, dst, axis, offset):
        place = next_sem[0]
        next_sem[0] = place + 1
        return pltpu.make_async_remote_copy(
            src_ref=src,
            dst_ref=dst,
            send_sem=send_sem.at[place],
            recv_sem=recv_sem.at[place],
            device_id={axis: along(axis, offset)},
            device_id_type=MESH,
        )

    unroll = 4

    def flux_chunk(chunk, _):
        ys = pl.ds(pl.multiple_of(chunk * 8, 8), 8)

        def cells(step, acc):
            acc = list(acc)
            for inner in range(unroll):
                x = step * unroll + inner
                w = [wtab[k, x] for k in range(6)]
                rho, energy = den[x, ys, :], ene[x, ys, :]
                m = [mom[j, x, ys, :] for j in range(3)]
                inverse = 1.0 / rho
                v = [m[j] * inverse for j in range(3)]
                own = [m[j] * v[j] for j in range(3)]
                pressure = (heat_ratio - 1.0) * (energy - 0.5 * (own[0] + own[1] + own[2]))
                m12, m13, m23 = m[0] * v[1], m[0] * v[2], m[1] * v[2]
                total = energy + pressure
                flux_x = (m[0], own[0] + pressure, m12, m13, total * v[0])
                flux_y = (m[1], m12, own[1] + pressure, m23, total * v[1])
                flux_z = (m[2], m13, m23, own[2] + pressure, total * v[2])
                state = (rho, m[0], m[1], m[2], energy)
                for f in range(fields):
                    fx[f, x, ys, :] = flux_x[f]
                    fy[f, x, ys, :] = flux_y[f]
                    fz[f, x, ys, :] = flux_z[f]
                    acc[f] = acc[f] + w[0] * state[f] + w[2] * flux_x[f]
                    acc[5 + f] = acc[5 + f] + w[1] * state[f] + w[3] * flux_x[f]
                    acc[10 + f] = acc[10 + f] + w[4] * flux_x[f]
                    acc[15 + f] = acc[15 + f] + w[5] * flux_x[f]
            return tuple(acc)

        zero = jnp.zeros((8, size_z), jnp.float32)
        acc = lax.fori_loop(0, size_x // unroll, cells, (zero,) * 20)
        for f in range(fields):
            uv0[0, f, ys, :] = acc[f]
            uv0[1, f, ys, :] = acc[5 + f]
            xn_out[0, 0, f, ys, :] = acc[10 + f]
            xn_out[0, 1, f, ys, :] = fx[f, size_x - 1, ys, :]
            xn_out[1, 0, f, ys, :] = acc[15 + f]
            xn_out[1, 1, f, ys, :] = fx[f, 0, ys, :]

        def sums(step, acc):
            acc = list(acc)
            for inner in range(unroll):
                x = step * unroll + inner
                w = [wtab[k, x] for k in range(2)]
                for f in range(fields):
                    value_y, value_z = fy[f, x, ys, :], fz[f, x, ys, :]
                    acc[f] = acc[f] + w[0] * value_y
                    acc[5 + f] = acc[5 + f] + w[1] * value_y
                    acc[10 + f] = acc[10 + f] + w[0] * value_z
                    acc[15 + f] = acc[15 + f] + w[1] * value_z
            return tuple(acc)

        acc = lax.fori_loop(0, size_x // unroll, sums, (zero,) * 20)
        for f in range(fields):
            sy[f, ys, :] = acc[f]
            sy[5 + f, ys, :] = acc[5 + f]
            sz[0, f, ys, :] = acc[10 + f]
            sz[1, f, ys, :] = acc[15 + f]
        return 0

    lax.fori_loop(0, size_y // 8, flux_chunk, 0)
    sy[10:16] = jnp.zeros((6, size_y, size_z), jnp.float32)
    sz[:, 5:8] = jnp.zeros((2, 3, size_y, size_z), jnp.float32)

    pl.semaphore_wait(barrier, nx + ny + nz - 3)

    xn = [
        remote(xn_out.at[0], xn_in.at[0], "gx", 1),
        remote(xn_out.at[1], xn_in.at[1], "gx", -1),
    ]
    for copy in xn:
        copy.start()
    for owner in range(nx):
        for side in range(2):
            for f in range(fields):
                xm_out[owner, side, rows * f : rows * f + rows, :] = xn_out[
                    side, 0, f, rows * owner : rows * owner + rows, :
                ]
    xm = [remote(xm_out.at[along("gx", k)], xm_in.at[k], "gx", k) for k in range(1, nx)]
    for copy in xm:
        copy.start()
    xm_in[0] = xm_out[me_x]

    for load in loads:
        load.wait()
    shape = (8 * size_y, ny * size_y)
    row_place = lax.broadcasted_iota(jnp.int32, shape, 0)
    col_place = lax.broadcasted_iota(jnp.int32, shape, 1)
    mine = col_place == me_y * size_y + lax.rem(row_place, size_y)
    metric_rows = jnp.sum(jnp.where(mine, metric[...], 0.0), axis=1, keepdims=True)
    ky[: 8 * size_y, :] = ky[: 8 * size_y, :] * metric_rows
    py[...] = py[...] * metric_rows

    def apply_wall(cells):
        result = jnp.dot(ky[...], cells, precision=HIGH, preferred_element_type=jnp.float32)
        return (
            result[: 8 * size_y].reshape(8, size_y, size_z),
            result[8 * size_y :].reshape(4, 8, size_z),
        )

    def span_moments(cells):
        return lax.dot_general(
            qz[...], cells, (((1,), (1,)), ((), ())), precision=HIGH, preferred_element_type=jnp.float32
        )

    for group in range(2):
        dys[8 * group : 8 * group + 8], ys_out[:, 8 * group : 8 * group + 8, :] = apply_wall(
            sy[8 * group : 8 * group + 8].reshape(8 * size_y, size_z)
        )
    ys = [
        remote(ys_out.at[pl.ds(0, 3)], ys_in.at[pl.ds(0, 3)], "gy", 1),
        remote(ys_out.at[pl.ds(1, 2)], ys_in.at[pl.ds(3, 2)], "gy", 2),
        remote(ys_out.at[pl.ds(1, 3)], ys_in.at[pl.ds(5, 3)], "gy", 3),
    ]
    for copy in ys:
        copy.start()
    zs_in[0] = span_moments(
        jnp.concatenate([sz[0].reshape(8 * size_y, size_z), sz[1].reshape(8 * size_y, size_z)], axis=1)
    )
    zs = [remote(zs_in.at[0], zs_in.at[k], "gz", k) for k in range(1, nz)]
    for copy in zs:
        copy.start()
    dzs[...] = jnp.dot(
        sz[...].reshape(16 * size_y, size_z), kz[...], precision=HIGH, preferred_element_type=jnp.float32
    ).reshape(2, 8, size_y, size_z)

    def wall_field(f, _):
        def wall_group(group, _):
            xs = pl.ds(pl.multiple_of(group * 8, 8), 8)
            local, moments = apply_wall(fy[f, xs].reshape(8 * size_y, size_z))
            tend[f, xs] = local
            yb_out[:, f, xs, :] = moments
            return 0

        return lax.fori_loop(0, size_x // 8, wall_group, 0)

    lax.fori_loop(0, fields, wall_field, 0)
    yb = [
        remote(yb_out.at[pl.ds(0, 3)], yb_in.at[pl.ds(0, 3)], "gy", 1),
        remote(yb_out.at[pl.ds(1, 2)], yb_in.at[pl.ds(3, 2)], "gy", 2),
        remote(yb_out.at[pl.ds(1, 3)], yb_in.at[pl.ds(5, 3)], "gy", 3),
    ]
    for copy in yb:
        copy.start()
    half = size_x // 2

    def span_field(f, _):
        pair = [fz[f, pl.ds(part * half, half)].reshape(half * size_y, size_z) for part in range(2)]
        zm_in[0, f] = span_moments(jnp.concatenate(pair, axis=1))
        return 0

    lax.fori_loop(0, fields, span_field, 0)
    zm = [remote(zm_in.at[0], zm_in.at[k], "gz", k) for k in range(1, nz)]
    for copy in zm:
        copy.start()

    def span_carries(received):
        return lax.dot_general(
            received, pz[...], (((0,), (0,)), ((), ())), precision=HIGH, preferred_element_type=jnp.float32
        )

    for copy in xn + ys + zs:
        copy.wait()
    powers = (ratio ** np.arange(size_x), ratio ** (size_x - 1.0 - np.arange(size_x)))
    span = span_carries(zs_in[...].reshape(8 * nz, 8 * size_y))
    wall = [
        jnp.dot(
            py[...],
            ys_in[:, 8 * group : 8 * group + 8, :].reshape(64, size_z),
            precision=HIGH,
            preferred_element_type=jnp.float32,
        )
        for group in range(2)
    ]
    for side in range(2):
        gains = [
            amplitude * float(weights[side] @ powers[0]),
            corner * float(weights[side][0]),
            -amplitude * float(weights[side] @ powers[1]),
            -corner * float(weights[side][size_x - 1]),
        ]
        for f in range(fields):
            unit = 5 * side + f
            place = (unit % 8) * size_y
            change = dys[unit] + wall[unit // 8][place : place + size_y]
            change = change + dzs[side, f] + span[f * size_y : (f + 1) * size_y, side * size_z : (side + 1) * size_z]
            for gain, value in zip(gains, (xn_in[0, 0, f], xn_in[0, 1, f], xn_in[1, 0, f], xn_in[1, 1, f])):
                change = change + gain * value
            value = uv0[side, f] - time_step * change
            for owner in range(nx):
                uv_out[owner, side, rows * f : rows * f + rows, :] = value[rows * owner : rows * owner + rows]
    uv = [remote(uv_out.at[along("gx", k)], uv_in.at[k], "gx", k) for k in range(1, nx)]
    for copy in uv:
        copy.start()
    uv_in[0] = uv_out[me_x]

    def sweep(behind, power, values):
        step = 1 if behind else -1
        total = values[0] if behind else values[nx - 1]
        for k in range(1, nx):
            total = total + float(power**k) * (values[k] if behind else values[nx - 1 - k])
        total = total * float(1.0 / (1.0 - power**nx))
        place = nx - 1 if behind else 0
        result = [None] * nx
        result[place] = total
        for _ in range(nx - 1):
            total = values[place] + float(power) * total
            place = place - step
            result[place] = total
        return result

    for copy in xm:
        copy.wait()
    power = ratio**size_x
    near_l = sweep(True, power, [xm_in[k, 0] for k in range(nx)])
    near_r = sweep(False, power, [xm_in[k, 1] for k in range(nx)])
    for k in range(nx):
        xo_out[k, 0] = float(power) * near_l[(k + 1) % nx]
        xo_out[k, 1] = float(power) * near_r[(k - 1) % nx]
    xo = [remote(xo_out.at[k], xo_in.at[me_x], "gx", -k) for k in range(1, nx)]
    for copy in xo:
        copy.start()
    xo_in[me_x] = xo_out[0]

    def span_local(f, _):
        for part in range(4):
            xs = pl.ds(part * (size_x // 4), size_x // 4)
            tend[f, xs] += jnp.dot(
                fz[f, xs].reshape(size_x // 4 * size_y, size_z),
                kz[...],
                precision=HIGH,
                preferred_element_type=jnp.float32,
            ).reshape(size_x // 4, size_y, size_z)
        return 0

    lax.fori_loop(0, fields, span_local, 0)

    for copy in uv:
        copy.wait()
    filter_power = filter_ratio**size_x
    for side in range(2):
        gain_l = -time_step * amplitude * float(weights[side] @ powers[0])
        gain_r = time_step * amplitude * float(weights[side] @ powers[1])
        values = [uv_in[k, side] + gain_l * xo_out[k, 0] + gain_r * xo_out[k, 1] for k in range(nx)]
        for k, value in enumerate(sweep(side == 0, filter_power, values)):
            io_out[k, side] = value
    io = [remote(io_out.at[k], io_in.at[me_x], "gx", -k) for k in range(1, nx)]
    for copy in io:
        copy.start()
    io_in[me_x] = io_out[0]

    for copy in yb + zm:
        copy.wait()

    def carries(f, _):
        for part in range(4):
            xs = pl.ds(8 * part, 8)
            tend[f, xs] += jnp.dot(
                py[...],
                yb_in[:, f, xs, :].reshape(64, size_z),
                precision=HIGH,
                preferred_element_type=jnp.float32,
            ).reshape(8, size_y, size_z)
        both = span_carries(zm_in[:, f].reshape(8 * nz, half * size_y))
        for part in range(2):
            xs = pl.ds(part * half, half)
            tend[f, xs] += both[:, part * size_z : (part + 1) * size_z].reshape(half, size_y, size_z)
        return 0

    lax.fori_loop(0, fields, carries, 0)

    def scan_chunk(chunk, _):
        ys = pl.ds(pl.multiple_of(chunk * 8, 8), 8)

        def ahead(step, carried):
            carried = list(carried)
            for inner in range(unroll):
                x = step * unroll + inner
                for f in range(fields):
                    u, before = carried[f], carried[5 + f]
                    tend[f, x, ys, :] += amplitude * u + corner * before
                    here = fx[f, x, ys, :]
                    carried[f], carried[5 + f] = ratio * (u + here), here
            return tuple(carried)

        def back(step, carried):
            carried = list(carried)
            for inner in range(unroll):
                x = size_x - 1 - (step * unroll + inner)
                for f in range(fields):
                    v, after = carried[f], carried[5 + f]
                    tend[f, x, ys, :] = amplitude * v + corner * after - tend[f, x, ys, :]
                    here = fx[f, x, ys, :]
                    carried[f], carried[5 + f] = ratio * (v + here), here
            return tuple(carried)

        for side, body in enumerate((ahead, back)):
            start = [xn_in[side, kind, f, ys, :] for kind in range(2) for f in range(fields)]
            lax.fori_loop(0, size_x // unroll, body, tuple(start))
        return 0

    lax.fori_loop(0, size_y // 8, scan_chunk, 0)

    for copy in xo + io:
        copy.wait()
    carry_x[...] = xo_in[...]
    carry_f[...] = io_in[...]


def filter_kernel(rows, den, mom, ene, part, carry_x, carry_f, wtab, tend, after, middle):
    fields, size_x = part.shape[:2]
    filter_ratio, gain = decay(filter_alpha)
    straight = 0.5 * (0.5 + filter_alpha) / filter_alpha
    amplitude = (0.5 + filter_alpha - straight) * gain
    unroll = 4

    def chunk(ref, side, f):
        return jnp.concatenate([ref[o, side, rows * f : rows * f + rows, :] for o in range(ref.shape[0])], axis=0)

    far_l = [chunk(carry_x, 0, f) for f in range(fields)]
    far_r = [chunk(carry_x, 1, f) for f in range(fields)]

    def ahead(step, carried):
        carried = list(carried)
        for inner in range(unroll):
            x = step * unroll + inner
            state = (den[x], mom[0, x], mom[1, x], mom[2, x], ene[x])
            gain_l, gain_r = wtab[6, x], wtab[7, x]
            for f in range(fields):
                rate = part[f, x] - gain_l * far_l[f] + gain_r * far_r[f]
                tend[f, x] = rate
                value = state[f] + time_step * rate
                middle[f, x] = value
                after[f, x] = (straight + amplitude) * value + amplitude * carried[f]
                carried[f] = filter_ratio * (carried[f] + value)
        return tuple(carried)

    def back(step, carried):
        carried = list(carried)
        for inner in range(unroll):
            x = size_x - 1 - (step * unroll + inner)
            for f in range(fields):
                after[f, x] += amplitude * carried[f]
                carried[f] = filter_ratio * (carried[f] + middle[f, x])
        return tuple(carried)

    for side, body in enumerate((ahead, back)):
        lax.fori_loop(0, size_x // unroll, body, tuple(chunk(carry_f, side, f) for f in range(fields)))


def solution(mesh):
    nx, ny, nz = mesh.shape["gx"], mesh.shape["gy"], mesh.shape["gz"]

    def on_device(density, momentum, energy, metric):
        size_x, size_y, size_z = density.shape
        fields = 5
        rows = size_y // nx
        float32 = jnp.float32
        ky, py = wall_tables(ny, size_y)
        kz, qz, pz = span_tables(nz, size_z)
        wtab = stream_weights(size_x).astype(np.float32)
        cells = (fields, size_x, size_y, size_z)
        owned = (nx, 2, fields * rows, size_z)
        vmem = pl.BlockSpec(memory_space=pltpu.VMEM)
        anywhere = pl.BlockSpec(memory_space=pl.ANY)
        copies = 2 + 4 * (nx - 1) + 6 + 2 * (nz - 1)
        part, carry_x, carry_f = pl.pallas_call(
            functools.partial(exchange_kernel, nx, ny, nz),
            out_shape=[
                jax.ShapeDtypeStruct(cells, float32),
                jax.ShapeDtypeStruct(owned, float32),
                jax.ShapeDtypeStruct(owned, float32),
            ],
            in_specs=[vmem, vmem, vmem, vmem, pl.BlockSpec(memory_space=pltpu.SMEM), anywhere, anywhere, vmem, vmem, vmem],
            out_specs=[vmem, vmem, vmem],
            scratch_shapes=[
                pltpu.VMEM(cells, float32),
                pltpu.VMEM(cells, float32),
                pltpu.VMEM(cells, float32),
                pltpu.VMEM(ky.shape[1:], float32),
                pltpu.VMEM(py.shape[1:], float32),
                pltpu.VMEM((2, fields, size_y, size_z), float32),
                pltpu.VMEM((16, size_y, size_z), float32),
                pltpu.VMEM((2, 8, size_y, size_z), float32),
                pltpu.VMEM((16, size_y, size_z), float32),
                pltpu.VMEM((2, 8, size_y, size_z), float32),
                pltpu.VMEM((4, 16, size_z), float32),
                pltpu.VMEM((8, 16, size_z), float32),
                pltpu.VMEM((nz, 8, 8 * size_y), float32),
                pltpu.VMEM((4, fields, size_x, size_z), float32),
                pltpu.VMEM((8, fields, size_x, size_z), float32),
                pltpu.VMEM((nz, fields, 8, size_x // 2 * size_y), float32),
                pltpu.VMEM((2, 2, fields, size_y, size_z), float32),
                pltpu.VMEM((2, 2, fields, size_y, size_z), float32),
                pltpu.VMEM(owned, float32),
                pltpu.VMEM(owned, float32),
                pltpu.VMEM(owned, float32),
                pltpu.VMEM(owned, float32),
                pltpu.VMEM(owned, float32),
                pltpu.VMEM(owned, float32),
                pltpu.VMEM(owned, float32),
                pltpu.VMEM(owned, float32),
                pltpu.SemaphoreType.DMA((2,)),
                pltpu.SemaphoreType.DMA((copies,)),
                pltpu.SemaphoreType.DMA((copies,)),
            ],
            compiler_params=pltpu.CompilerParams(
                collective_id=0, has_side_effects=True, vmem_limit_bytes=48 * 1024 * 1024
            ),
            cost_estimate=pl.CostEstimate(flops=4 * 10**9, bytes_accessed=10**7, transcendentals=0),
        )(
            density,
            momentum,
            energy,
            metric.reshape(1, -1),
            jnp.asarray(wtab),
            jnp.asarray(ky),
            jnp.asarray(py),
            jnp.asarray(kz),
            jnp.asarray(qz),
            jnp.asarray(pz),
        )
        owners = 8 // rows
        field_block = pl.BlockSpec((fields, size_x, 8, size_z), lambda i: (0, 0, i, 0))
        scalar_block = pl.BlockSpec((size_x, 8, size_z), lambda i: (0, i, 0))
        carry_block = pl.BlockSpec((owners, 2, fields * rows, size_z), lambda i: (i, 0, 0, 0))
        return pl.pallas_call(
            functools.partial(filter_kernel, rows),
            grid=(size_y // 8,),
            out_shape=[jax.ShapeDtypeStruct(cells, float32), jax.ShapeDtypeStruct(cells, float32)],
            in_specs=[
                scalar_block,
                pl.BlockSpec((3, size_x, 8, size_z), lambda i: (0, 0, i, 0)),
                scalar_block,
                field_block,
                carry_block,
                carry_block,
                pl.BlockSpec(memory_space=pltpu.SMEM),
            ],
            out_specs=[field_block, field_block],
            scratch_shapes=[pltpu.VMEM((fields, size_x, 8, size_z), float32)],
            compiler_params=pltpu.CompilerParams(vmem_limit_bytes=32 * 1024 * 1024),
            cost_estimate=pl.CostEstimate(flops=10**7, bytes_accessed=10**7, transcendentals=0),
        )(density, momentum, energy, part, carry_x, carry_f, jnp.asarray(wtab))

    return jax.shard_map(
        on_device,
        mesh=mesh,
        in_specs=(P("gx", "gy", "gz"), P(None, "gx", "gy", "gz"), P("gx", "gy", "gz"), P()),
        out_specs=(P(None, "gx", "gy", "gz"), P(None, "gx", "gy", "gz")),
        check_vma=False,
    )
```

profile of v0, /device:TPU:1, one launch (start us, length us, event | category | flops | bytes accessed | tf_op | source)
XLA Modules:
  0.0 57.6 jit_solution(10614241653424033779)
XLA Ops:
  0.6 0.0 copy-start.1
  0.6 1.4 %copy-done.1 = f32[3,32,32,128]{3,2,1,0:T(8,128)S(1)} copy-done((f32[3,32,32,128]{3,2,1,0:T(8,128)S(1)}, f32[3,32,32,128]{3,2,1,0:T(8,128)}, u32[]{:S(2)}) %copy-start.1) | copy-done | bytes 1572888
  2.0 0.0 copy-start.2
  2.0 1.0 %copy-done.2 = f32[32,32,128]{2,1,0:T(8,128)S(1)} copy-done((f32[32,32,128]{2,1,0:T(8,128)S(1)}, f32[32,32,128]{2,1,0:T(8,128)}, u32[]{:S(2)}) %copy-start.2) | copy-done | bytes 524312
  3.1 0.0 copy-start.3
  3.1 1.0 %copy-done.3 = f32[32,32,128]{2,1,0:T(8,128)S(1)} copy-done((f32[32,32,128]{2,1,0:T(8,128)S(1)}, f32[32,32,128]{2,1,0:T(8,128)}, u32[]{:S(2)}) %copy-start.3) | copy-done | bytes 524312
  4.1 0.0 copy-start.4
  4.1 0.7 %copy-done.4 = f32[8,32]{1,0:T(8,128)S(1)} copy-done((f32[8,32]{1,0:T(8,128)S(1)}, f32[8,32]{1,0:T(8,128)}, u32[]{:S(2)}) %copy-start.4) | copy-done | bytes 1048
  4.8 0.0 copy-start.5
  4.8 0.7 %copy-done.5 = f32[128]{0:T(128)S(1)} copy-done((f32[128]{0:T(128)S(1)}, f32[128]{0:T(128)}, u32[]{:S(2)}) %copy-start.5) | copy-done | bytes 536
  5.5 0.0 copy-start.6
  5.5 1.3 %copy-done.6 = f32[4,288,256]{2,1,0:T(8,128)S(1)} copy-done((f32[4,288,256]{2,1,0:T(8,128)S(1)}, f32[4,288,256]{2,1,0:T(8,128)}, u32[]{:S(2)}) %copy-start.6) | copy-done | bytes 1179672
  6.7 0.0 copy-start.7
  6.7 1.0 %copy-done.7 = f32[4,256,64]{2,1,0:T(8,128)S(1)} copy-done((f32[4,256,64]{2,1,0:T(8,128)S(1)}, f32[4,256,64]{2,1,0:T(8,128)}, u32[]{:S(2)}) %copy-start.7) | copy-done | bytes 262168
  7.8 0.0 copy-start.8
  7.8 0.8 %copy-done.8 = f32[128,128]{1,0:T(8,128)S(1)} copy-done((f32[128,128]{1,0:T(8,128)S(1)}, f32[128,128]{1,0:T(8,128)}, u32[]{:S(2)}) %copy-start.8) | copy-done | bytes 65560
  8.6 0.0 copy-start.9
  8.6 0.8 %copy-done.9 = f32[32,256]{1,0:T(8,128)S(1)} copy-done((f32[32,256]{1,0:T(8,128)S(1)}, f32[32,256]{1,0:T(8,128)}, u32[]{:S(2)}) %copy-start.9) | copy-done | bytes 32792
  9.4 0.0 copy-start.10
  9.4 0.7 %copy-done.10 = f32[8,256]{1,0:T(8,128)S(1)} copy-done((f32[8,256]{1,0:T(8,128)S(1)}, f32[8,256]{1,0:T(8,128)}, u32[]{:S(2)}) %copy-start.10) | copy-done | bytes 8216
  10.1 40.9 %shard_map.113 = (f32[5,32,32,128]{3,2,1,0:T(8,128)}, f32[16,2,10,128]{3,2,1,0:T(8,128)S(1)}, f32[16,2,10,128]{3,2,1,0:T(8,128)S(1)}) custom-call(f32[32,32,128]{2,1,0:T(8,128)S(1)} %copy-done.2, f32[3,32,32,128]{3,2,1,0:T(8,128)S(1)} %copy-done.1, f32[32,32,128]{2,1,0:T(8,128)S(1)} %copy-done.3, f32[1,128]{1,0:T(1,128)S(1)} %bitcast.1, ...), custom_call_target="tpu_custom_call" | custom-call | flops 4000000000 | bytes 10000000 | tf_op jit(solution)/shard_map/pallas_call | solution.py:659
  51.0 0.0 copy-start
  51.0 1.7 %copy-done = f32[5,32,32,128]{3,2,1,0:T(8,128)S(1)} copy-done((f32[5,32,32,128]{3,2,1,0:T(8,128)S(1)}, f32[5,32,32,128]{3,2,1,0:T(8,128)}, u32[]{:S(2)}) %copy-start) | copy-done | bytes 2621464
  52.7 4.9 %shard_map.114 = (f32[5,32,32,128]{3,2,1,0:T(8,128)}, f32[5,32,32,128]{3,2,1,0:T(8,128)}) custom-call(f32[32,32,128]{2,1,0:T(8,128)S(1)} %copy-done.2, f32[3,32,32,128]{3,2,1,0:T(8,128)S(1)} %copy-done.1, f32[32,32,128]{2,1,0:T(8,128)S(1)} %copy-done.3, f32[5,32,32,128]{3,2,1,0:T(8,128)S(1)} %copy-done, f32[16,2,10,128]{3,2,1,0:T(8,128)S(1)} %get-tuple-element.6.carry_x, ...), custom_call_target="tpu_custom_call" | custom-call | flops 10000000 | bytes 10000000 | tf_op jit(solution)/shard_map/pallas_call | solution.py:719
Async XLA Ops:
  0.6 1.4 %copy-start.1 = (f32[3,32,32,128]{3,2,1,0:T(8,128)S(1)}, f32[3,32,32,128]{3,2,1,0:T(8,128)}, u32[]{:S(2)}) copy-start(f32[3,32,32,128]{3,2,1,0:T(8,128)} %mom.3) | copy-start | bytes 4718596
  2.0 1.0 %copy-start.2 = (f32[32,32,128]{2,1,0:T(8,128)S(1)}, f32[32,32,128]{2,1,0:T(8,128)}, u32[]{:S(2)}) copy-start(f32[32,32,128]{2,1,0:T(8,128)} %den.3) | copy-start | bytes 1572868
  3.1 1.0 %copy-start.3 = (f32[32,32,128]{2,1,0:T(8,128)S(1)}, f32[32,32,128]{2,1,0:T(8,128)}, u32[]{:S(2)}) copy-start(f32[32,32,128]{2,1,0:T(8,128)} %ene.3) | copy-start | bytes 1572868
  4.1 0.7 %copy-start.4 = (f32[8,32]{1,0:T(8,128)S(1)}, f32[8,32]{1,0:T(8,128)}, u32[]{:S(2)}) copy-start(f32[8,32]{1,0:T(8,128)} %constant.12.clone.wtab) | copy-start | bytes 3076
  4.8 0.7 %copy-start.5 = (f32[128]{0:T(128)S(1)}, f32[128]{0:T(128)}, u32[]{:S(2)}) copy-start(f32[128]{0:T(128)} %param.13) | copy-start | bytes 1540
  5.5 1.3 %copy-start.6 = (f32[4,288,256]{2,1,0:T(8,128)S(1)}, f32[4,288,256]{2,1,0:T(8,128)}, u32[]{:S(2)}) copy-start(f32[4,288,256]{2,1,0:T(8,128)} %constant.13.clone.ky_hbm) | copy-start | bytes 3538948
  6.7 1.0 %copy-start.7 = (f32[4,256,64]{2,1,0:T(8,128)S(1)}, f32[4,256,64]{2,1,0:T(8,128)}, u32[]{:S(2)}) copy-start(f32[4,256,64]{2,1,0:T(8,128)} %constant.14.clone.py_hbm) | copy-start | bytes 786436
  7.8 0.8 %copy-start.8 = (f32[128,128]{1,0:T(8,128)S(1)}, f32[128,128]{1,0:T(8,128)}, u32[]{:S(2)}) copy-start(f32[128,128]{1,0:T(8,128)} %constant.15.clone.kz) | copy-start | bytes 196612
  8.6 0.8 %copy-start.9 = (f32[32,256]{1,0:T(8,128)S(1)}, f32[32,256]{1,0:T(8,128)}, u32[]{:S(2)}) copy-start(f32[32,256]{1,0:T(8,128)} %constant.17.clone.pz) | copy-start | bytes 98308
  9.4 0.7 %copy-start.10 = (f32[8,256]{1,0:T(8,128)S(1)}, f32[8,256]{1,0:T(8,128)}, u32[]{:S(2)}) copy-start(f32[8,256]{1,0:T(8,128)} %constant.16.clone.qz) | copy-start | bytes 24580
  51.0 1.7 %copy-start = (f32[5,32,32,128]{3,2,1,0:T(8,128)S(1)}, f32[5,32,32,128]{3,2,1,0:T(8,128)}, u32[]{:S(2)}) copy-start(f32[5,32,32,128]{3,2,1,0:T(8,128)} %get-tuple-element.5.part) | copy-start | bytes 7864324
where the time goes:
time: 58.1 us; the launch traced here: 57.6 us
  Pallas kernels  45.8 us (79%)
  local copies, waits for them, and re-layouts  11.2 us (19%)
  between operations  0.66 us (1%)
    pallas_call x1, Pallas kernels, on_device(): pl.pallas_call(functools.partial(exchange_kernel, nx, ny, nz), out_shape=...  40.9 us
    unnamed x22, local copies, waits for them, and re-layouts  11.2 us
    pallas_call x1, Pallas kernels, on_device(): pl.pallas_call(functools.partial(filter_kernel, rows), grid=(size_y // 8,...  4.89 us

commit v1 on v0

--- a/solution.py
+++ b/solution.py
@@ -14,7 +14,7 @@
 time_step = 0.05
 near_weight = 7.0 / 9.0
 wide_weight = 1.0 / 36.0
-HIGH = lax.Precision.HIGHEST
+bfloat16 = jnp.bfloat16
 MESH = pl.DeviceIdType.MESH
 KINDS_Y = ((1, "last"), (1, "ml"), (1, "mr"), (2, "ml"), (2, "mr"), (3, "ml"), (3, "mr"), (3, "first"))
 
@@ -146,7 +146,12 @@
                 elif kind == "first" and distance == 1:
                     column[size - 1] = corner_r[b]
             carry[b, :, 8 * place : 8 * place + 8] = np.kron(eye, column[:, None])
-    return apply.astype(np.float32), carry.astype(np.float32)
+    return apply.astype(np.float32), np.concatenate([carry] * 3, axis=2).astype(np.float32)
+
+
+def table_split(table):
+    high = table.astype(bfloat16)
+    return high, (table - high.astype(np.float64)).astype(bfloat16)
 
 
 @functools.cache
@@ -175,10 +180,12 @@
     both_carries = np.zeros((blocks, 8, 2 * size))
     both_carries[:, :4, :size] = carries
     both_carries[:, 4:, size:] = carries
+    local_high, local_low = table_split(local_compact(size).T)
+    carry_high, carry_low = table_split(both_carries.reshape(8 * blocks, 2 * size))
     return (
-        local_compact(size).T.astype(np.float32),
-        both_moments.astype(np.float32),
-        both_carries.reshape(8 * blocks, 2 * size).astype(np.float32),
+        np.block([[local_high, local_low], [local_high, np.zeros_like(local_low)]]),
+        np.concatenate(table_split(both_moments)),
+        np.concatenate([carry_high, carry_high, carry_low]),
     )
 
 
@@ -197,34 +204,52 @@
             -time_step * (weight_v @ local),
             ratio ** (size - places),
             ratio ** (places + 1.0),
-            amplitude * ratio**places,
-            amplitude * ratio ** (size - 1.0 - places),
         ]
     )
+
+
+def split(values):
+    high = values.astype(bfloat16)
+    return high, (values - high.astype(jnp.float32)).astype(bfloat16)
+
+
+def product(left, right, sides=((1,), (0,))):
+    return lax.dot_general(left, right, (sides, ((), ())), preferred_element_type=jnp.float32)
 
 
 def exchange_kernel(
     nx,
     ny,
     nz,
+    den_hbm,
+    mom_hbm,
+    ene_hbm,
+    metric_hbm,
+    wtab_hbm,
+    ky_hbm,
+    py_hbm,
+    kz_hbm,
+    qz_hbm,
+    pz_hbm,
+    tend,
+    carry_x,
+    carry_f,
     den,
     mom,
     ene,
     metric,
     wtab,
-    ky_hbm,
-    py_hbm,
+    ky,
+    py,
     kz,
     qz,
     pz,
-    tend,
-    carry_x,
-    carry_f,
+    ky_high,
+    ky_low,
+    py_both,
     fx,
     fy,
     fz,
-    ky,
-    py,
     uv0,
     sy,
     sz,
@@ -261,17 +286,19 @@
         me, count = {"gx": (me_x, nx), "gy": (me_y, ny), "gz": (me_z, nz)}[axis]
         return lax.rem(me + offset + count, count)
 
+    sources = (wtab_hbm, den_hbm, mom_hbm, ene_hbm, ky_hbm.at[me_y], py_hbm.at[me_y], metric_hbm, kz_hbm, qz_hbm, pz_hbm)
+    targets = (wtab, den, mom, ene, ky, py, metric, kz, qz, pz)
+    loads = [
+        pltpu.make_async_copy(source, target, load_sem.at[place])
+        for place, (source, target) in enumerate(zip(sources, targets))
+    ]
+    for load in loads:
+        load.start()
+
     barrier = pltpu.get_barrier_semaphore()
     for axis, count in (("gx", nx), ("gy", ny), ("gz", nz)):
         for offset in range(1, count):
             pl.semaphore_signal(barrier, inc=1, device_id={axis: along(axis, offset)}, device_id_type=MESH)
-
-    loads = [
-        pltpu.make_async_copy(ky_hbm.at[me_y], ky, load_sem.at[0]),
-        pltpu.make_async_copy(py_hbm.at[me_y], py, load_sem.at[1]),
-    ]
-    for load in loads:
-        load.start()
 
     next_sem = [0]
 
@@ -286,6 +313,9 @@
             device_id={axis: along(axis, offset)},
             device_id_type=MESH,
         )
+
+    for load in loads[:4]:
+        load.wait()
 
     unroll = 4
 
@@ -373,7 +403,7 @@
         copy.start()
     xm_in[0] = xm_out[me_x]
 
-    for load in loads:
+    for load in loads[4:]:
         load.wait()
     shape = (8 * size_y, ny * size_y)
     row_place = lax.broadcasted_iota(jnp.int32, shape, 0)
@@ -381,24 +411,46 @@
     mine = col_place == me_y * size_y + lax.rem(row_place, size_y)
     metric_rows = jnp.sum(jnp.where(mine, metric[...], 0.0), axis=1, keepdims=True)
     ky[: 8 * size_y, :] = ky[: 8 * size_y, :] * metric_rows
-    py[...] = py[...] * metric_rows
-
-    def apply_wall(cells):
-        result = jnp.dot(ky[...], cells, precision=HIGH, preferred_element_type=jnp.float32)
-        return (
-            result[: 8 * size_y].reshape(8, size_y, size_z),
-            result[8 * size_y :].reshape(4, 8, size_z),
+    ky_high[...], ky_low[...] = split(ky[...])
+    high, low = split(py[...] * metric_rows)
+    py_both[...] = jnp.where(lax.broadcasted_iota(jnp.int32, py.shape, 1) < 128, high, low)
+
+    def apply_wall(first, second):
+        cells = jnp.concatenate(
+            [first.reshape(8 * size_y, size_z), second.reshape(8 * size_y, size_z)], axis=1
         )
-
-    def span_moments(cells):
-        return lax.dot_general(
-            qz[...], cells, (((1,), (1,)), ((), ())), precision=HIGH, preferred_element_type=jnp.float32
-        )
-
-    for group in range(2):
-        dys[8 * group : 8 * group + 8], ys_out[:, 8 * group : 8 * group + 8, :] = apply_wall(
-            sy[8 * group : 8 * group + 8].reshape(8 * size_y, size_z)
-        )
+        high, low = split(cells)
+        result = product(ky_high[...], high) + product(ky_high[...], low) + product(ky_low[...], high)
+        return [
+            (
+                result[: 8 * size_y, lanes].reshape(8, size_y, size_z),
+                result[8 * size_y :, lanes].reshape(4, 8, size_z),
+            )
+            for lanes in (slice(0, size_z), slice(size_z, 2 * size_z))
+        ]
+
+    def wall_carries(first, second):
+        cells = jnp.concatenate([first.reshape(64, size_z), second.reshape(64, size_z)], axis=1)
+        high, low = split(cells)
+        return product(py_both[...], jnp.concatenate([high, low, high], axis=0))
+
+    def span_local(cells):
+        result = product(jnp.concatenate(split(cells), axis=1), kz[...])
+        return result[:, :size_z] + result[:, size_z:]
+
+    def span_moments(first, second):
+        high, low = split(jnp.concatenate([first, second], axis=1))
+        from_high = product(qz[...], high, ((1,), (1,)))
+        from_low = product(qz[...], low, ((1,), (1,)))
+        return from_high[:8] + from_high[8:] + (from_low[:8] + from_low[8:])
+
+    def span_carries(received):
+        high, low = split(received)
+        return product(jnp.concatenate([high, low, high], axis=0), pz[...], ((0,), (0,)))
+
+    for group, (local, moments) in enumerate(apply_wall(sy[0:8], sy[8:16])):
+        dys[8 * group : 8 * group + 8] = local
+        ys_out[:, 8 * group : 8 * group + 8, :] = moments
     ys = [
         remote(ys_out.at[pl.ds(0, 3)], ys_in.at[pl.ds(0, 3)], "gy", 1),
         remote(ys_out.at[pl.ds(1, 2)], ys_in.at[pl.ds(3, 2)], "gy", 2),
@@ -406,25 +458,19 @@
     ]
     for copy in ys:
         copy.start()
-    zs_in[0] = span_moments(
-        jnp.concatenate([sz[0].reshape(8 * size_y, size_z), sz[1].reshape(8 * size_y, size_z)], axis=1)
-    )
+    zs_in[0] = span_moments(sz[0].reshape(8 * size_y, size_z), sz[1].reshape(8 * size_y, size_z))
     zs = [remote(zs_in.at[0], zs_in.at[k], "gz", k) for k in range(1, nz)]
     for copy in zs:
         copy.start()
-    dzs[...] = jnp.dot(
-        sz[...].reshape(16 * size_y, size_z), kz[...], precision=HIGH, preferred_element_type=jnp.float32
-    ).reshape(2, 8, size_y, size_z)
+    dzs[...] = span_local(sz[...].reshape(16 * size_y, size_z)).reshape(2, 8, size_y, size_z)
 
     def wall_field(f, _):
-        def wall_group(group, _):
-            xs = pl.ds(pl.multiple_of(group * 8, 8), 8)
-            local, moments = apply_wall(fy[f, xs].reshape(8 * size_y, size_z))
-            tend[f, xs] = local
-            yb_out[:, f, xs, :] = moments
-            return 0
-
-        return lax.fori_loop(0, size_x // 8, wall_group, 0)
+        for part in range(size_x // 16):
+            pair = [pl.ds(16 * part + 8 * side, 8) for side in range(2)]
+            for xs, (local, moments) in zip(pair, apply_wall(fy[f, pair[0]], fy[f, pair[1]])):
+                tend[f, xs] = local
+                yb_out[:, f, xs, :] = moments
+        return 0
 
     lax.fori_loop(0, fields, wall_field, 0)
     yb = [
@@ -438,32 +484,19 @@
 
     def span_field(f, _):
         pair = [fz[f, pl.ds(part * half, half)].reshape(half * size_y, size_z) for part in range(2)]
-        zm_in[0, f] = span_moments(jnp.concatenate(pair, axis=1))
+        zm_in[0, f] = span_moments(*pair)
         return 0
 
     lax.fori_loop(0, fields, span_field, 0)
     zm = [remote(zm_in.at[0], zm_in.at[k], "gz", k) for k in range(1, nz)]
     for copy in zm:
         copy.start()
-
-    def span_carries(received):
-        return lax.dot_general(
-            received, pz[...], (((0,), (0,)), ((), ())), precision=HIGH, preferred_element_type=jnp.float32
-        )
 
     for copy in xn + ys + zs:
         copy.wait()
     powers = (ratio ** np.arange(size_x), ratio ** (size_x - 1.0 - np.arange(size_x)))
     span = span_carries(zs_in[...].reshape(8 * nz, 8 * size_y))
-    wall = [
-        jnp.dot(
-            py[...],
-            ys_in[:, 8 * group : 8 * group + 8, :].reshape(64, size_z),
-            precision=HIGH,
-            preferred_element_type=jnp.float32,
-        )
-        for group in range(2)
-    ]
+    wall = wall_carries(ys_in[:, 0:8, :], ys_in[:, 8:16, :])
     for side in range(2):
         gains = [
             amplitude * float(weights[side] @ powers[0]),
@@ -473,8 +506,8 @@
         ]
         for f in range(fields):
             unit = 5 * side + f
-            place = (unit % 8) * size_y
-            change = dys[unit] + wall[unit // 8][place : place + size_y]
+            place, lane = (unit % 8) * size_y, (unit // 8) * size_z
+            change = dys[unit] + wall[place : place + size_y, lane : lane + size_z]
             change = change + dzs[side, f] + span[f * size_y : (f + 1) * size_y, side * size_z : (side + 1) * size_z]
             for gain, value in zip(gains, (xn_in[0, 0, f], xn_in[0, 1, f], xn_in[1, 0, f], xn_in[1, 1, f])):
                 change = change + gain * value
@@ -514,18 +547,36 @@
         copy.start()
     xo_in[me_x] = xo_out[0]
 
-    def span_local(f, _):
-        for part in range(4):
-            xs = pl.ds(part * (size_x // 4), size_x // 4)
-            tend[f, xs] += jnp.dot(
-                fz[f, xs].reshape(size_x // 4 * size_y, size_z),
-                kz[...],
-                precision=HIGH,
-                preferred_element_type=jnp.float32,
-            ).reshape(size_x // 4, size_y, size_z)
+    def span_cells(f, _):
+        for part in range(size_x // 8):
+            xs = pl.ds(8 * part, 8)
+            tend[f, xs] += span_local(fz[f, xs].reshape(8 * size_y, size_z)).reshape(8, size_y, size_z)
         return 0
 
-    lax.fori_loop(0, fields, span_local, 0)
+    lax.fori_loop(0, fields, span_cells, 0)
+
+    def scan_chunk(chunk, _):
+        ys = pl.ds(pl.multiple_of(chunk * 8, 8), 8)
+
+        def scan(side, step, carried):
+            carried = list(carried)
+            for inner in range(unroll):
+                x = step * unroll + inner
+                x = size_x - 1 - x if side else x
+                gains = (-amplitude, -corner) if side else (amplitude, corner)
+                for f in range(fields):
+                    total, last = carried[f], carried[5 + f]
+                    tend[f, x, ys, :] += gains[0] * total + gains[1] * last
+                    here = fx[f, x, ys, :]
+                    carried[f], carried[5 + f] = ratio * (total + here), here
+            return tuple(carried)
+
+        for side in range(2):
+            start = [xn_in[side, kind, f, ys, :] for kind in range(2) for f in range(fields)]
+            lax.fori_loop(0, size_x // unroll, functools.partial(scan, side), tuple(start))
+        return 0
+
+    lax.fori_loop(0, size_y // 8, scan_chunk, 0)
 
     for copy in uv:
         copy.wait()
@@ -545,53 +596,19 @@
         copy.wait()
 
     def carries(f, _):
-        for part in range(4):
-            xs = pl.ds(8 * part, 8)
-            tend[f, xs] += jnp.dot(
-                py[...],
-                yb_in[:, f, xs, :].reshape(64, size_z),
-                precision=HIGH,
-                preferred_element_type=jnp.float32,
-            ).reshape(8, size_y, size_z)
         both = span_carries(zm_in[:, f].reshape(8 * nz, half * size_y))
-        for part in range(2):
-            xs = pl.ds(part * half, half)
-            tend[f, xs] += both[:, part * size_z : (part + 1) * size_z].reshape(half, size_y, size_z)
+        for part in range(size_x // 16):
+            pair = [pl.ds(16 * part + 8 * side, 8) for side in range(2)]
+            wall = wall_carries(yb_in[:, f, pair[0], :], yb_in[:, f, pair[1], :])
+            for side, xs in enumerate(pair):
+                row = (16 * part + 8 * side) % half * size_y
+                lane = (16 * part + 8 * side) // half * size_z
+                change = wall[:, side * size_z : (side + 1) * size_z]
+                change = change + both[row : row + 8 * size_y, lane : lane + size_z]
+                tend[f, xs] += change.reshape(8, size_y, size_z)
         return 0
 
     lax.fori_loop(0, fields, carries, 0)
-
-    def scan_chunk(chunk, _):
-        ys = pl.ds(pl.multiple_of(chunk * 8, 8), 8)
-
-        def ahead(step, carried):
-            carried = list(carried)
-            for inner in range(unroll):
-                x = step * unroll + inner
-                for f in range(fields):
-                    u, before = carried[f], carried[5 + f]
-                    tend[f, x, ys, :] += amplitude * u + corner * before
-                    here = fx[f, x, ys, :]
-                    carried[f], carried[5 + f] = ratio * (u + here), here
-            return tuple(carried)
-
-        def back(step, carried):
-            carried = list(carried)
-            for inner in range(unroll):
-                x = size_x - 1 - (step * unroll + inner)
-                for f in range(fields):
-                    v, after = carried[f], carried[5 + f]
-                    tend[f, x, ys, :] = amplitude * v + corner * after - tend[f, x, ys, :]
-                    here = fx[f, x, ys, :]
-                    carried[f], carried[5 + f] = ratio * (v + here), here
-            return tuple(carried)
-
-        for side, body in enumerate((ahead, back)):
-            start = [xn_in[side, kind, f, ys, :] for kind in range(2) for f in range(fields)]
-            lax.fori_loop(0, size_x // unroll, body, tuple(start))
-        return 0
-
-    lax.fori_loop(0, size_y // 8, scan_chunk, 0)
 
     for copy in xo + io:
         copy.wait()
@@ -599,7 +616,7 @@
     carry_f[...] = io_in[...]
 
 
-def filter_kernel(rows, den, mom, ene, part, carry_x, carry_f, wtab, tend, after, middle):
+def filter_kernel(rows, den, mom, ene, part, carry_x, carry_f, tend, after, middle):
     fields, size_x = part.shape[:2]
     filter_ratio, gain = decay(filter_alpha)
     straight = 0.5 * (0.5 + filter_alpha) / filter_alpha
@@ -609,17 +626,20 @@
     def chunk(ref, side, f):
         return jnp.concatenate([ref[o, side, rows * f : rows * f + rows, :] for o in range(ref.shape[0])], axis=0)
 
-    far_l = [chunk(carry_x, 0, f) for f in range(fields)]
-    far_r = [chunk(carry_x, 1, f) for f in range(fields)]
+    ratio, far_gain, _ = compact_kernel()
+    start = [chunk(carry_f, 0, f) for f in range(fields)]
+    start += [far_gain * chunk(carry_x, 0, f) for f in range(fields)]
+    start += [float(far_gain * ratio ** (size_x - 1)) * chunk(carry_x, 1, f) for f in range(fields)]
 
     def ahead(step, carried):
         carried = list(carried)
         for inner in range(unroll):
             x = step * unroll + inner
             state = (den[x], mom[0, x], mom[1, x], mom[2, x], ene[x])
-            gain_l, gain_r = wtab[6, x], wtab[7, x]
             for f in range(fields):
-                rate = part[f, x] - gain_l * far_l[f] + gain_r * far_r[f]
+                far_l, far_r = carried[5 + f], carried[10 + f]
+                rate = far_r - far_l - part[f, x]
+                carried[5 + f], carried[10 + f] = ratio * far_l, (1.0 / ratio) * far_r
                 tend[f, x] = rate
                 value = state[f] + time_step * rate
                 middle[f, x] = value
@@ -636,8 +656,8 @@
                 carried[f] = filter_ratio * (carried[f] + middle[f, x])
         return tuple(carried)
 
-    for side, body in enumerate((ahead, back)):
-        lax.fori_loop(0, size_x // unroll, body, tuple(chunk(carry_f, side, f) for f in range(fields)))
+    lax.fori_loop(0, size_x // unroll, ahead, tuple(start))
+    lax.fori_loop(0, size_x // unroll, back, tuple(chunk(carry_f, 1, f) for f in range(fields)))
 
 
 def solution(mesh):
@@ -654,7 +674,7 @@
         cells = (fields, size_x, size_y, size_z)
         owned = (nx, 2, fields * rows, size_z)
         vmem = pl.BlockSpec(memory_space=pltpu.VMEM)
-        anywhere = pl.BlockSpec(memory_space=pl.ANY)
+        stays = pl.BlockSpec(memory_space=pltpu.HBM)
         copies = 2 + 4 * (nx - 1) + 6 + 2 * (nz - 1)
         part, carry_x, carry_f = pl.pallas_call(
             functools.partial(exchange_kernel, nx, ny, nz),
@@ -663,14 +683,25 @@
                 jax.ShapeDtypeStruct(owned, float32),
                 jax.ShapeDtypeStruct(owned, float32),
             ],
-            in_specs=[vmem, vmem, vmem, vmem, pl.BlockSpec(memory_space=pltpu.SMEM), anywhere, anywhere, vmem, vmem, vmem],
+            in_specs=[stays] * 10,
             out_specs=[vmem, vmem, vmem],
             scratch_shapes=[
+                pltpu.VMEM(cells[1:], float32),
+                pltpu.VMEM((3,) + cells[1:], float32),
+                pltpu.VMEM(cells[1:], float32),
+                pltpu.VMEM((1, ny * size_y), float32),
+                pltpu.SMEM(wtab.shape, float32),
+                pltpu.VMEM(ky.shape[1:], float32),
+                pltpu.VMEM(py.shape[1:], float32),
+                pltpu.VMEM(kz.shape, bfloat16),
+                pltpu.VMEM(qz.shape, bfloat16),
+                pltpu.VMEM(pz.shape, bfloat16),
+                pltpu.VMEM(ky.shape[1:], bfloat16),
+                pltpu.VMEM(ky.shape[1:], bfloat16),
+                pltpu.VMEM(py.shape[1:], bfloat16),
                 pltpu.VMEM(cells, float32),
                 pltpu.VMEM(cells, float32),
                 pltpu.VMEM(cells, float32),
-                pltpu.VMEM(ky.shape[1:], float32),
-                pltpu.VMEM(py.shape[1:], float32),
                 pltpu.VMEM((2, fields, size_y, size_z), float32),
                 pltpu.VMEM((16, size_y, size_z), float32),
                 pltpu.VMEM((2, 8, size_y, size_z), float32),
@@ -692,25 +723,19 @@
                 pltpu.VMEM(owned, float32),
                 pltpu.VMEM(owned, float32),
                 pltpu.VMEM(owned, float32),
-                pltpu.SemaphoreType.DMA((2,)),
+                pltpu.SemaphoreType.DMA((10,)),
                 pltpu.SemaphoreType.DMA((copies,)),
                 pltpu.SemaphoreType.DMA((copies,)),
             ],
             compiler_params=pltpu.CompilerParams(
-                collective_id=0, has_side_effects=True, vmem_limit_bytes=48 * 1024 * 1024
+                collective_id=0, has_side_effects=True, vmem_limit_bytes=24 * 1024 * 1024
             ),
             cost_estimate=pl.CostEstimate(flops=4 * 10**9, bytes_accessed=10**7, transcendentals=0),
         )(
-            density,
-            momentum,
-            energy,
-            metric.reshape(1, -1),
-            jnp.asarray(wtab),
-            jnp.asarray(ky),
-            jnp.asarray(py),
-            jnp.asarray(kz),
-            jnp.asarray(qz),
-            jnp.asarray(pz),
+            *[
+                pltpu.with_memory_space_constraint(jnp.asarray(value), pltpu.HBM)
+                for value in (density, momentum, energy, metric.reshape(1, -1), wtab, ky, py, kz, qz, pz)
+            ]
         )
         owners = 8 // rows
         field_block = pl.BlockSpec((fields, size_x, 8, size_z), lambda i: (0, 0, i, 0))
@@ -727,13 +752,12 @@
                 field_block,
                 carry_block,
                 carry_block,
-                pl.BlockSpec(memory_space=pltpu.SMEM),
             ],
             out_specs=[field_block, field_block],
             scratch_shapes=[pltpu.VMEM((fields, size_x, 8, size_z), float32)],
-            compiler_params=pltpu.CompilerParams(vmem_limit_bytes=32 * 1024 * 1024),
+            compiler_params=pltpu.CompilerParams(vmem_limit_bytes=12 * 1024 * 1024),
             cost_estimate=pl.CostEstimate(flops=10**7, bytes_accessed=10**7, transcendentals=0),
-        )(density, momentum, energy, part, carry_x, carry_f, jnp.asarray(wtab))
+        )(density, momentum, energy, part, carry_x, carry_f)
 
     return jax.shard_map(
         on_device,

time: 58.1 us -> 35.3 us (0.61)
  Pallas kernels: 45.8 us -> 34.5 us
  local copies, waits for them, and re-layouts: 11.2 us -> 0.01 us
    unnamed x22 -> x6, local copies, waits for them, and re-layouts: 11.2 us -> 0.01 us
    pallas_call x1, Pallas kernels: 40.9 us -> 30.1 us  [on_device(): pl.pallas_call(functools.partial(exchange_kernel, nx, ny, nz), out_shape=...]
where the time goes in v1:
time: 35.3 us; the launch traced here: 35.2 us
  Pallas kernels  34.5 us (98%)
  between operations  0.69 us (2%)
    pallas_call x1, Pallas kernels, on_device(): pl.pallas_call(functools.partial(exchange_kernel, nx, ny, nz), out_shape=...  30.1 us
    pallas_call x1, Pallas kernels, on_device(): pl.pallas_call(functools.partial(filter_kernel, rows), grid=(size_y // 8,...  4.38 us

profile of v1, /device:TPU:1, one launch (start us, length us, event | category | flops | bytes accessed | tf_op | source)
XLA Modules:
  0.0 35.2 jit_solution(8987569696231024386)
XLA Ops:
  0.6 0.0 copy-start
  0.6 0.0 copy-start.1
  0.7 0.0 copy-start.2
  0.7 30.1 %shard_map.113 = (f32[5,32,32,128]{3,2,1,0:T(8,128)S(1)}, f32[16,2,10,128]{3,2,1,0:T(8,128)S(1)}, f32[16,2,10,128]{3,2,1,0:T(8,128)S(1)}) custom-call(f32[32,32,128]{2,1,0:T(8,128)} %den.1, f32[3,32,32,128]{3,2,1,0:T(8,128)} %mom.1, f32[32,32,128]{2,1,0:T(8,128)} %ene.1, f32[1,128]{1,0:T(1,128)} %bitcast.1, f32[6,32]{1,0:T(8,128)} %constant.12.clone.wtab_hbm, ...), custom_call_target="tpu_custom_call" | custom-call | flops 4000000000 | bytes 10000000 | tf_op jit(solution)/shard_map/pallas_call | solution.py:679
  30.8 0.0 copy-done
  30.8 0.0 copy-done.1
  30.8 0.0 copy-done.2
  30.8 4.4 %shard_map.114 = (f32[5,32,32,128]{3,2,1,0:T(8,128)}, f32[5,32,32,128]{3,2,1,0:T(8,128)}) custom-call(f32[32,32,128]{2,1,0:T(8,128)S(1)} %copy-done.1, f32[3,32,32,128]{3,2,1,0:T(8,128)S(1)} %copy-done, f32[32,32,128]{2,1,0:T(8,128)S(1)} %copy-done.2, f32[5,32,32,128]{3,2,1,0:T(8,128)S(1)} %get-tuple-element.5.part, ...), custom_call_target="tpu_custom_call" | custom-call | flops 10000000 | bytes 10000000 | tf_op jit(solution)/shard_map/pallas_call | solution.py:744
Async XLA Ops:
  0.6 30.2 %copy-start = (f32[3,32,32,128]{3,2,1,0:T(8,128)S(1)}, f32[3,32,32,128]{3,2,1,0:T(8,128)}, u32[]{:S(2)}) copy-start(f32[3,32,32,128]{3,2,1,0:T(8,128)} %mom.1) | copy-start | bytes 4718596
  0.6 30.2 %copy-start.1 = (f32[32,32,128]{2,1,0:T(8,128)S(1)}, f32[32,32,128]{2,1,0:T(8,128)}, u32[]{:S(2)}) copy-start(f32[32,32,128]{2,1,0:T(8,128)} %den.1) | copy-start | bytes 1572868
  0.7 30.2 %copy-start.2 = (f32[32,32,128]{2,1,0:T(8,128)S(1)}, f32[32,32,128]{2,1,0:T(8,128)}, u32[]{:S(2)}) copy-start(f32[32,32,128]{2,1,0:T(8,128)} %ene.1) | copy-start | bytes 1572868

commit v2 on v1

--- a/solution.py
+++ b/solution.py
@@ -190,22 +190,25 @@
 
 
 def stream_weights(size):
-    ratio, amplitude, _ = compact_kernel()
+    ratio, _, _ = compact_kernel()
     filter_ratio, _ = decay(filter_alpha)
     places = np.arange(size)
-    weight_u = filter_ratio ** (size - places)
-    weight_v = filter_ratio ** (places + 1.0)
-    local = local_compact(size)
     return np.stack(
         [
-            weight_u,
-            weight_v,
-            -time_step * (weight_u @ local),
-            -time_step * (weight_v @ local),
+            filter_ratio ** (size - places),
+            filter_ratio ** (places + 1.0),
             ratio ** (size - places),
             ratio ** (places + 1.0),
         ]
     )
+
+
+def filtered_derivative():
+    ratio, amplitude, corner = compact_kernel()
+    filter_ratio, _ = decay(filter_alpha)
+    over, times = ratio / filter_ratio, ratio * filter_ratio
+    gain = amplitude * (over / (1.0 - over) - times / (1.0 - times)) + corner * (1.0 / filter_ratio - filter_ratio)
+    return gain, amplitude / (1.0 - over), amplitude * filter_ratio / (1.0 - times), corner, corner * filter_ratio
 
 
 def split(values):
@@ -234,6 +237,7 @@
     tend,
     carry_x,
     carry_f,
+    carry_d,
     den,
     mom,
     ene,
@@ -271,6 +275,7 @@
     xo_in,
     io_out,
     io_in,
+    state_sem,
     load_sem,
     send_sem,
     recv_sem,
@@ -279,20 +284,34 @@
     me_x, me_y, me_z = lax.axis_index("gx"), lax.axis_index("gy"), lax.axis_index("gz")
     rows = size_y // nx
     ratio, amplitude, corner = compact_kernel()
-    weights = stream_weights(size_x)
     filter_ratio, _ = decay(filter_alpha)
+    gain_d, near_d, far_d, corner_d, first_d = filtered_derivative()
+    half_rows = fields * rows
+    farthest = sorted(range(1, nx), key=lambda k: -min(k, nx - k))
 
     def along(axis, offset):
         me, count = {"gx": (me_x, nx), "gy": (me_y, ny), "gz": (me_z, nz)}[axis]
         return lax.rem(me + offset + count, count)
 
-    sources = (wtab_hbm, den_hbm, mom_hbm, ene_hbm, ky_hbm.at[me_y], py_hbm.at[me_y], metric_hbm, kz_hbm, qz_hbm, pz_hbm)
-    targets = (wtab, den, mom, ene, ky, py, metric, kz, qz, pz)
+    def state_loads(chunk):
+        ys = pl.ds(pl.multiple_of(chunk * 8, 8), 8)
+        return [
+            pltpu.make_async_copy(den_hbm.at[:, ys], den.at[:, ys], state_sem.at[0, chunk]),
+            pltpu.make_async_copy(mom_hbm.at[:, :, ys], mom.at[:, :, ys], state_sem.at[1, chunk]),
+            pltpu.make_async_copy(ene_hbm.at[:, ys], ene.at[:, ys], state_sem.at[2, chunk]),
+        ]
+
+    sources = (wtab_hbm, ky_hbm.at[me_y], py_hbm.at[me_y], metric_hbm, kz_hbm, qz_hbm, pz_hbm)
+    targets = (wtab, ky, py, metric, kz, qz, pz)
     loads = [
         pltpu.make_async_copy(source, target, load_sem.at[place])
         for place, (source, target) in enumerate(zip(sources, targets))
     ]
-    for load in loads:
+    loads[0].start()
+    for chunk in range(size_y // 8):
+        for load in state_loads(chunk):
+            load.start()
+    for load in loads[1:]:
         load.start()
 
     barrier = pltpu.get_barrier_semaphore()
@@ -314,19 +333,21 @@
             device_id_type=MESH,
         )
 
-    for load in loads[:4]:
-        load.wait()
+    loads[0].wait()
 
     unroll = 4
+    zero = jnp.zeros((8, size_z), jnp.float32)
 
     def flux_chunk(chunk, _):
         ys = pl.ds(pl.multiple_of(chunk * 8, 8), 8)
+        for load in state_loads(chunk):
+            load.wait()
 
         def cells(step, acc):
             acc = list(acc)
             for inner in range(unroll):
                 x = step * unroll + inner
-                w = [wtab[k, x] for k in range(6)]
+                w = [wtab[k, x] for k in range(2)]
                 rho, energy = den[x, ys, :], ene[x, ys, :]
                 m = [mom[j, x, ys, :] for j in range(3)]
                 inverse = 1.0 / rho
@@ -338,41 +359,17 @@
                 flux_x = (m[0], own[0] + pressure, m12, m13, total * v[0])
                 flux_y = (m[1], m12, own[1] + pressure, m23, total * v[1])
                 flux_z = (m[2], m13, m23, own[2] + pressure, total * v[2])
-                state = (rho, m[0], m[1], m[2], energy)
                 for f in range(fields):
                     fx[f, x, ys, :] = flux_x[f]
                     fy[f, x, ys, :] = flux_y[f]
                     fz[f, x, ys, :] = flux_z[f]
-                    acc[f] = acc[f] + w[0] * state[f] + w[2] * flux_x[f]
-                    acc[5 + f] = acc[5 + f] + w[1] * state[f] + w[3] * flux_x[f]
-                    acc[10 + f] = acc[10 + f] + w[4] * flux_x[f]
-                    acc[15 + f] = acc[15 + f] + w[5] * flux_x[f]
+                    acc[f] = acc[f] + w[0] * flux_y[f]
+                    acc[5 + f] = acc[5 + f] + w[1] * flux_y[f]
+                    acc[10 + f] = acc[10 + f] + w[0] * flux_z[f]
+                    acc[15 + f] = acc[15 + f] + w[1] * flux_z[f]
             return tuple(acc)
 
-        zero = jnp.zeros((8, size_z), jnp.float32)
         acc = lax.fori_loop(0, size_x // unroll, cells, (zero,) * 20)
-        for f in range(fields):
-            uv0[0, f, ys, :] = acc[f]
-            uv0[1, f, ys, :] = acc[5 + f]
-            xn_out[0, 0, f, ys, :] = acc[10 + f]
-            xn_out[0, 1, f, ys, :] = fx[f, size_x - 1, ys, :]
-            xn_out[1, 0, f, ys, :] = acc[15 + f]
-            xn_out[1, 1, f, ys, :] = fx[f, 0, ys, :]
-
-        def sums(step, acc):
-            acc = list(acc)
-            for inner in range(unroll):
-                x = step * unroll + inner
-                w = [wtab[k, x] for k in range(2)]
-                for f in range(fields):
-                    value_y, value_z = fy[f, x, ys, :], fz[f, x, ys, :]
-                    acc[f] = acc[f] + w[0] * value_y
-                    acc[5 + f] = acc[5 + f] + w[1] * value_y
-                    acc[10 + f] = acc[10 + f] + w[0] * value_z
-                    acc[15 + f] = acc[15 + f] + w[1] * value_z
-            return tuple(acc)
-
-        acc = lax.fori_loop(0, size_x // unroll, sums, (zero,) * 20)
         for f in range(fields):
             sy[f, ys, :] = acc[f]
             sy[5 + f, ys, :] = acc[5 + f]
@@ -380,30 +377,11 @@
             sz[1, f, ys, :] = acc[15 + f]
         return 0
 
-    lax.fori_loop(0, size_y // 8, flux_chunk, 0)
     sy[10:16] = jnp.zeros((6, size_y, size_z), jnp.float32)
     sz[:, 5:8] = jnp.zeros((2, 3, size_y, size_z), jnp.float32)
-
-    pl.semaphore_wait(barrier, nx + ny + nz - 3)
-
-    xn = [
-        remote(xn_out.at[0], xn_in.at[0], "gx", 1),
-        remote(xn_out.at[1], xn_in.at[1], "gx", -1),
-    ]
-    for copy in xn:
-        copy.start()
-    for owner in range(nx):
-        for side in range(2):
-            for f in range(fields):
-                xm_out[owner, side, rows * f : rows * f + rows, :] = xn_out[
-                    side, 0, f, rows * owner : rows * owner + rows, :
-                ]
-    xm = [remote(xm_out.at[along("gx", k)], xm_in.at[k], "gx", k) for k in range(1, nx)]
-    for copy in xm:
-        copy.start()
-    xm_in[0] = xm_out[me_x]
-
-    for load in loads[4:]:
+    lax.fori_loop(0, size_y // 8, flux_chunk, 0)
+
+    for load in loads[1:]:
         load.wait()
     shape = (8 * size_y, ny * size_y)
     row_place = lax.broadcasted_iota(jnp.int32, shape, 0)
@@ -447,6 +425,8 @@
     def span_carries(received):
         high, low = split(received)
         return product(jnp.concatenate([high, low, high], axis=0), pz[...], ((0,), (0,)))
+
+    pl.semaphore_wait(barrier, nx + ny + nz - 3)
 
     for group, (local, moments) in enumerate(apply_wall(sy[0:8], sy[8:16])):
         dys[8 * group : 8 * group + 8] = local
@@ -464,6 +444,36 @@
         copy.start()
     dzs[...] = span_local(sz[...].reshape(16 * size_y, size_z)).reshape(2, 8, size_y, size_z)
 
+    def stream_chunk(chunk, _):
+        ys = pl.ds(pl.multiple_of(chunk * 8, 8), 8)
+
+        def sums(step, acc):
+            acc = list(acc)
+            for inner in range(unroll):
+                x = step * unroll + inner
+                w = [wtab[k, x] for k in range(4)]
+                state = (den[x, ys, :], mom[0, x, ys, :], mom[1, x, ys, :], mom[2, x, ys, :], ene[x, ys, :])
+                for f in range(fields):
+                    flux = fx[f, x, ys, :]
+                    change = (time_step * gain_d) * flux
+                    acc[f] = acc[f] + w[0] * (state[f] - change)
+                    acc[5 + f] = acc[5 + f] + w[1] * (state[f] + change)
+                    acc[10 + f] = acc[10 + f] + w[2] * flux
+                    acc[15 + f] = acc[15 + f] + w[3] * flux
+            return tuple(acc)
+
+        acc = lax.fori_loop(0, size_x // unroll, sums, (zero,) * 20)
+        for f in range(fields):
+            uv0[0, f, ys, :] = acc[f]
+            uv0[1, f, ys, :] = acc[5 + f]
+            xn_out[0, 0, f, ys, :] = acc[10 + f]
+            xn_out[0, 1, f, ys, :] = fx[f, size_x - 1, ys, :]
+            xn_out[1, 0, f, ys, :] = acc[15 + f]
+            xn_out[1, 1, f, ys, :] = fx[f, 0, ys, :]
+        return 0
+
+    lax.fori_loop(0, size_y // 8, stream_chunk, 0)
+
     def wall_field(f, _):
         for part in range(size_x // 16):
             pair = [pl.ds(16 * part + 8 * side, 8) for side in range(2)]
@@ -480,44 +490,65 @@
     ]
     for copy in yb:
         copy.start()
-    half = size_x // 2
-
-    def span_field(f, _):
-        pair = [fz[f, pl.ds(part * half, half)].reshape(half * size_y, size_z) for part in range(2)]
-        zm_in[0, f] = span_moments(*pair)
-        return 0
-
-    lax.fori_loop(0, fields, span_field, 0)
-    zm = [remote(zm_in.at[0], zm_in.at[k], "gz", k) for k in range(1, nz)]
-    for copy in zm:
-        copy.start()
-
-    for copy in xn + ys + zs:
+
+    def span_carries(received):
+        high, low = split(received)
+        return product(jnp.concatenate([high, low, high], axis=0), pz[...], ((0,), (0,)))
+
+    def deal(message, side, f, values):
+        for owner in range(nx):
+            place = side * half_rows + rows * f
+            message[owner, place : place + rows, :] = values[rows * owner : rows * owner + rows]
+
+    for copy in ys + zs:
         copy.wait()
-    powers = (ratio ** np.arange(size_x), ratio ** (size_x - 1.0 - np.arange(size_x)))
     span = span_carries(zs_in[...].reshape(8 * nz, 8 * size_y))
     wall = wall_carries(ys_in[:, 0:8, :], ys_in[:, 8:16, :])
     for side in range(2):
-        gains = [
-            amplitude * float(weights[side] @ powers[0]),
-            corner * float(weights[side][0]),
-            -amplitude * float(weights[side] @ powers[1]),
-            -corner * float(weights[side][size_x - 1]),
-        ]
         for f in range(fields):
             unit = 5 * side + f
             place, lane = (unit % 8) * size_y, (unit // 8) * size_z
             change = dys[unit] + wall[place : place + size_y, lane : lane + size_z]
             change = change + dzs[side, f] + span[f * size_y : (f + 1) * size_y, side * size_z : (side + 1) * size_z]
-            for gain, value in zip(gains, (xn_in[0, 0, f], xn_in[0, 1, f], xn_in[1, 0, f], xn_in[1, 1, f])):
-                change = change + gain * value
-            value = uv0[side, f] - time_step * change
-            for owner in range(nx):
-                uv_out[owner, side, rows * f : rows * f + rows, :] = value[rows * owner : rows * owner + rows]
-    uv = [remote(uv_out.at[along("gx", k)], uv_in.at[k], "gx", k) for k in range(1, nx)]
+            deal(uv_out, side, f, uv0[side, f] - time_step * change)
+    uv = [remote(uv_out.at[along("gx", k)], uv_in.at[k], "gx", k) for k in farthest]
     for copy in uv:
         copy.start()
     uv_in[0] = uv_out[me_x]
+
+    xn = [
+        remote(xn_out.at[0], xn_in.at[0], "gx", 1),
+        remote(xn_out.at[1], xn_in.at[1], "gx", -1),
+    ]
+    for copy in xn:
+        copy.start()
+    for side in range(2):
+        for f in range(fields):
+            deal(xm_out, side, f, xn_out[side, 0, f])
+    xm = [remote(xm_out.at[along("gx", k)], xm_in.at[k], "gx", k) for k in farthest]
+    for copy in xm:
+        copy.start()
+    xm_in[0] = xm_out[me_x]
+
+    half = size_x // 2
+
+    def span_field(f, _):
+        pair = [fz[f, pl.ds(part * half, half)].reshape(half * size_y, size_z) for part in range(2)]
+        zm_in[0, f] = span_moments(*pair)
+        return 0
+
+    lax.fori_loop(0, fields, span_field, 0)
+    zm = [remote(zm_in.at[0], zm_in.at[k], "gz", k) for k in range(1, nz)]
+    for copy in zm:
+        copy.start()
+
+    def span_cells(f, _):
+        for part in range(size_x // 8):
+            xs = pl.ds(8 * part, 8)
+            tend[f, xs] += span_local(fz[f, xs].reshape(8 * size_y, size_z)).reshape(8, size_y, size_z)
+        return 0
+
+    lax.fori_loop(0, fields, span_cells, 0)
 
     def sweep(behind, power, values):
         step = 1 if behind else -1
@@ -534,26 +565,20 @@
             result[place] = total
         return result
 
+    from_behind = lax.broadcasted_iota(jnp.int32, (2 * half_rows, size_z), 0) < half_rows
     for copy in xm:
         copy.wait()
     power = ratio**size_x
-    near_l = sweep(True, power, [xm_in[k, 0] for k in range(nx)])
-    near_r = sweep(False, power, [xm_in[k, 1] for k in range(nx)])
+    values = [xm_in[k] for k in range(nx)]
+    near_l, near_r = sweep(True, power, values), sweep(False, power, values)
     for k in range(nx):
-        xo_out[k, 0] = float(power) * near_l[(k + 1) % nx]
-        xo_out[k, 1] = float(power) * near_r[(k - 1) % nx]
-    xo = [remote(xo_out.at[k], xo_in.at[me_x], "gx", -k) for k in range(1, nx)]
+        xo_out[k] = float(power) * jnp.where(from_behind, near_l[(k + 1) % nx], near_r[(k - 1) % nx])
+    xo = [remote(xo_out.at[k], xo_in.at[me_x], "gx", -k) for k in farthest]
     for copy in xo:
         copy.start()
     xo_in[me_x] = xo_out[0]
-
-    def span_cells(f, _):
-        for part in range(size_x // 8):
-            xs = pl.ds(8 * part, 8)
-            tend[f, xs] += span_local(fz[f, xs].reshape(8 * size_y, size_z)).reshape(8, size_y, size_z)
-        return 0
-
-    lax.fori_loop(0, fields, span_cells, 0)
+    for copy in xn:
+        copy.wait()
 
     def scan_chunk(chunk, _):
         ys = pl.ds(pl.multiple_of(chunk * 8, 8), 8)
@@ -581,16 +606,25 @@
     for copy in uv:
         copy.wait()
     filter_power = filter_ratio**size_x
-    for side in range(2):
-        gain_l = -time_step * amplitude * float(weights[side] @ powers[0])
-        gain_r = time_step * amplitude * float(weights[side] @ powers[1])
-        values = [uv_in[k, side] + gain_l * xo_out[k, 0] + gain_r * xo_out[k, 1] for k in range(nx)]
-        for k, value in enumerate(sweep(side == 0, filter_power, values)):
-            io_out[k, side] = value
-    io = [remote(io_out.at[k], io_in.at[me_x], "gx", -k) for k in range(1, nx)]
+    values = [uv_in[k] for k in range(nx)]
+    filter_l, filter_r = sweep(True, filter_power, values), sweep(False, filter_power, values)
+    for k in range(nx):
+        io_out[k] = jnp.where(from_behind, filter_l[k], filter_r[k])
+    io = [remote(io_out.at[k], io_in.at[me_x], "gx", -k) for k in farthest]
     for copy in io:
         copy.start()
     io_in[me_x] = io_out[0]
+
+    for side in range(2):
+        sign = -time_step if side else time_step
+        for f in range(fields):
+            past = xn_out[1 - side, 0, f] + float(power) * xn_in[1 - side, 0, f]
+            carry_d[side, f] = (
+                (sign * near_d) * xn_in[side, 0, f]
+                + (sign * corner_d) * xn_in[side, 1, f]
+                + (sign * far_d) * past
+                + (sign * first_d) * xn_out[1 - side, 1, f]
+            )
 
     for copy in yb + zm:
         copy.wait()
@@ -616,48 +650,89 @@
     carry_f[...] = io_in[...]
 
 
-def filter_kernel(rows, den, mom, ene, part, carry_x, carry_f, tend, after, middle):
-    fields, size_x = part.shape[:2]
+def filter_kernel(den, mom, ene, part, carry_x, carry_f, carry_d, tend_hbm, after_hbm, tend, after, sems):
+    chunks, fields, size_x = tend.shape[:3]
+    half_rows = carry_x.shape[1] // 2
+    rows = half_rows // fields
+    owners = 8 // rows
+    ratio, far_gain, _ = compact_kernel()
     filter_ratio, gain = decay(filter_alpha)
     straight = 0.5 * (0.5 + filter_alpha) / filter_alpha
     amplitude = (0.5 + filter_alpha - straight) * gain
+    _, near_d, far_d, _, _ = filtered_derivative()
+    power = ratio**size_x
     unroll = 4
 
-    def chunk(ref, side, f):
-        return jnp.concatenate([ref[o, side, rows * f : rows * f + rows, :] for o in range(ref.shape[0])], axis=0)
-
-    ratio, far_gain, _ = compact_kernel()
-    start = [chunk(carry_f, 0, f) for f in range(fields)]
-    start += [far_gain * chunk(carry_x, 0, f) for f in range(fields)]
-    start += [float(far_gain * ratio ** (size_x - 1)) * chunk(carry_x, 1, f) for f in range(fields)]
-
-    def ahead(step, carried):
-        carried = list(carried)
-        for inner in range(unroll):
-            x = step * unroll + inner
-            state = (den[x], mom[0, x], mom[1, x], mom[2, x], ene[x])
-            for f in range(fields):
-                far_l, far_r = carried[5 + f], carried[10 + f]
-                rate = far_r - far_l - part[f, x]
-                carried[5 + f], carried[10 + f] = ratio * far_l, (1.0 / ratio) * far_r
-                tend[f, x] = rate
-                value = state[f] + time_step * rate
-                middle[f, x] = value
-                after[f, x] = (straight + amplitude) * value + amplitude * carried[f]
-                carried[f] = filter_ratio * (carried[f] + value)
-        return tuple(carried)
-
-    def back(step, carried):
-        carried = list(carried)
-        for inner in range(unroll):
-            x = size_x - 1 - (step * unroll + inner)
-            for f in range(fields):
-                after[f, x] += amplitude * carried[f]
-                carried[f] = filter_ratio * (carried[f] + middle[f, x])
-        return tuple(carried)
-
-    lax.fori_loop(0, size_x // unroll, ahead, tuple(start))
-    lax.fori_loop(0, size_x // unroll, back, tuple(chunk(carry_f, 1, f) for f in range(fields)))
+    def copies(chunk):
+        ys = pl.ds(pl.multiple_of(chunk * 8, 8), 8)
+        return (
+            pltpu.make_async_copy(tend.at[chunk], tend_hbm.at[:, :, ys], sems.at[0, chunk]),
+            pltpu.make_async_copy(after.at[chunk], after_hbm.at[:, :, ys], sems.at[1, chunk]),
+        )
+
+    def chunk_body(chunk, _):
+        ys = pl.ds(pl.multiple_of(chunk * 8, 8), 8)
+
+        def carried_in(ref, side, f):
+            place = side * half_rows + rows * f
+            return jnp.concatenate(
+                [ref[chunk * owners + o, place : place + rows, :] for o in range(owners)], axis=0
+            )
+
+        def state(f, x):
+            return den[x, ys, :] if f == 0 else ene[x, ys, :] if f == 4 else mom[f - 1, x, ys, :]
+
+        far_l = [carried_in(carry_x, 0, f) for f in range(fields)]
+        far_r = [carried_in(carry_x, 1, f) for f in range(fields)]
+        start_l = [
+            carried_in(carry_f, 0, f)
+            + carry_d[0, f, ys, :]
+            + time_step * (near_d * far_l[f] + float(far_d * power) * far_r[f])
+            for f in range(fields)
+        ]
+        start_r = [
+            carried_in(carry_f, 1, f)
+            + carry_d[1, f, ys, :]
+            - time_step * (near_d * far_r[f] + float(far_d * power) * far_l[f])
+            for f in range(fields)
+        ]
+        head = [float(far_gain * ratio ** (size_x - 1)) * far_l[f] for f in range(fields)]
+        tail = [far_gain * far_r[f] for f in range(fields)]
+
+        def back(step, carried):
+            carried = list(carried)
+            for inner in range(unroll):
+                x = size_x - 1 - (step * unroll + inner)
+                for f in range(fields):
+                    behind, ahead = carried[5 + f], carried[10 + f]
+                    rate = ahead - behind - part[f, x, ys, :]
+                    tend[chunk, f, x] = rate
+                    after[chunk, f, x] = amplitude * carried[f]
+                    carried[f] = filter_ratio * (carried[f] + (state(f, x) + time_step * rate))
+                    carried[5 + f], carried[10 + f] = (1.0 / ratio) * behind, ratio * ahead
+            return tuple(carried)
+
+        def ahead(step, carried):
+            carried = list(carried)
+            for inner in range(unroll):
+                x = step * unroll + inner
+                for f in range(fields):
+                    middle = state(f, x) + time_step * tend[chunk, f, x]
+                    after[chunk, f, x] += (straight + amplitude) * middle + amplitude * carried[f]
+                    carried[f] = filter_ratio * (carried[f] + middle)
+            return tuple(carried)
+
+        lax.fori_loop(0, size_x // unroll, back, tuple(start_r + head + tail))
+        rate_copy, after_copy = copies(chunk)
+        rate_copy.start()
+        lax.fori_loop(0, size_x // unroll, ahead, tuple(start_l))
+        after_copy.start()
+        return 0
+
+    lax.fori_loop(0, chunks, chunk_body, 0)
+    for chunk in range(chunks):
+        for copy in copies(chunk):
+            copy.wait()
 
 
 def solution(mesh):
@@ -672,19 +747,22 @@
         kz, qz, pz = span_tables(nz, size_z)
         wtab = stream_weights(size_x).astype(np.float32)
         cells = (fields, size_x, size_y, size_z)
-        owned = (nx, 2, fields * rows, size_z)
+        owned = (nx, 2 * fields * rows, size_z)
+        sides = (2, fields, size_y, size_z)
         vmem = pl.BlockSpec(memory_space=pltpu.VMEM)
         stays = pl.BlockSpec(memory_space=pltpu.HBM)
         copies = 2 + 4 * (nx - 1) + 6 + 2 * (nz - 1)
-        part, carry_x, carry_f = pl.pallas_call(
+        chunks = size_y // 8
+        part, carry_x, carry_f, carry_d = pl.pallas_call(
             functools.partial(exchange_kernel, nx, ny, nz),
             out_shape=[
                 jax.ShapeDtypeStruct(cells, float32),
                 jax.ShapeDtypeStruct(owned, float32),
                 jax.ShapeDtypeStruct(owned, float32),
+                jax.ShapeDtypeStruct(sides, float32),
             ],
             in_specs=[stays] * 10,
-            out_specs=[vmem, vmem, vmem],
+            out_specs=[vmem] * 4,
             scratch_shapes=[
                 pltpu.VMEM(cells[1:], float32),
                 pltpu.VMEM((3,) + cells[1:], float32),
@@ -702,7 +780,7 @@
                 pltpu.VMEM(cells, float32),
                 pltpu.VMEM(cells, float32),
                 pltpu.VMEM(cells, float32),
-                pltpu.VMEM((2, fields, size_y, size_z), float32),
+                pltpu.VMEM(sides, float32),
                 pltpu.VMEM((16, size_y, size_z), float32),
                 pltpu.VMEM((2, 8, size_y, size_z), float32),
                 pltpu.VMEM((16, size_y, size_z), float32),
@@ -723,7 +801,8 @@
                 pltpu.VMEM(owned, float32),
                 pltpu.VMEM(owned, float32),
                 pltpu.VMEM(owned, float32),
-                pltpu.SemaphoreType.DMA((10,)),
+                pltpu.SemaphoreType.DMA((3, chunks)),
+                pltpu.SemaphoreType.DMA((7,)),
                 pltpu.SemaphoreType.DMA((copies,)),
                 pltpu.SemaphoreType.DMA((copies,)),
             ],
@@ -737,27 +816,19 @@
                 for value in (density, momentum, energy, metric.reshape(1, -1), wtab, ky, py, kz, qz, pz)
             ]
         )
-        owners = 8 // rows
-        field_block = pl.BlockSpec((fields, size_x, 8, size_z), lambda i: (0, 0, i, 0))
-        scalar_block = pl.BlockSpec((size_x, 8, size_z), lambda i: (0, i, 0))
-        carry_block = pl.BlockSpec((owners, 2, fields * rows, size_z), lambda i: (i, 0, 0, 0))
         return pl.pallas_call(
-            functools.partial(filter_kernel, rows),
-            grid=(size_y // 8,),
+            filter_kernel,
             out_shape=[jax.ShapeDtypeStruct(cells, float32), jax.ShapeDtypeStruct(cells, float32)],
-            in_specs=[
-                scalar_block,
-                pl.BlockSpec((3, size_x, 8, size_z), lambda i: (0, 0, i, 0)),
-                scalar_block,
-                field_block,
-                carry_block,
-                carry_block,
+            in_specs=[vmem] * 7,
+            out_specs=[stays] * 2,
+            scratch_shapes=[
+                pltpu.VMEM((chunks, fields, size_x, 8, size_z), float32),
+                pltpu.VMEM((chunks, fields, size_x, 8, size_z), float32),
+                pltpu.SemaphoreType.DMA((2, chunks)),
             ],
-            out_specs=[field_block, field_block],
-            scratch_shapes=[pltpu.VMEM((fields, size_x, 8, size_z), float32)],
-            compiler_params=pltpu.CompilerParams(vmem_limit_bytes=12 * 1024 * 1024),
+            compiler_params=pltpu.CompilerParams(vmem_limit_bytes=16 * 1024 * 1024),
             cost_estimate=pl.CostEstimate(flops=10**7, bytes_accessed=10**7, transcendentals=0),
-        )(density, momentum, energy, part, carry_x, carry_f)
+        )(density, momentum, energy, part, carry_x, carry_f, carry_d)
 
     return jax.shard_map(
         on_device,

time: 35.3 us -> 39.8 us (1.13)
  Pallas kernels: 34.5 us -> 39 us
    pallas_call x1, Pallas kernels: 30.1 us -> 35.8 us  [on_device(): pl.pallas_call(functools.partial(exchange_kernel, nx, ny, nz), out_shape=...]
    pallas_call x1, Pallas kernels: 4.38 us -> 3.14 us  [on_device(): pl.pallas_call(filter_kernel, out_shape=[jax.ShapeDtypeStruct(cells, floa...]
where the time goes in v2:
time: 39.8 us; the launch traced here: 39.7 us
  Pallas kernels  39 us (98%)
  between operations  0.69 us (2%)
    pallas_call x1, Pallas kernels, on_device(): pl.pallas_call(functools.partial(exchange_kernel, nx, ny, nz), out_shape=...  35.8 us
    pallas_call x1, Pallas kernels, on_device(): pl.pallas_call(filter_kernel, out_shape=[jax.ShapeDtypeStruct(cells, floa...  3.14 us

profile of v2, /device:TPU:1, one launch (start us, length us, event | category | flops | bytes accessed | tf_op | source)
XLA Modules:
  0.0 39.7 jit_solution(8340583681937133064)
XLA Ops:
  0.6 0.0 copy-start
  0.6 0.0 copy-start.1
  0.7 0.0 copy-start.2
  0.7 35.8 %shard_map.113 = (f32[5,32,32,128]{3,2,1,0:T(8,128)S(1)}, f32[16,20,128]{2,1,0:T(8,128)S(1)}, f32[16,20,128]{2,1,0:T(8,128)S(1)}, f32[2,5,32,128]{3,2,1,0:T(8,128)S(1)}) custom-call(f32[32,32,128]{2,1,0:T(8,128)} %den.1, f32[3,32,32,128]{3,2,1,0:T(8,128)} %mom.1, f32[32,32,128]{2,1,0:T(8,128)} %ene.1, f32[1,128]{1,0:T(1,128)} %bitcast.1, ...), custom_call_target="tpu_custom_call" | custom-call | flops 4000000000 | bytes 10000000 | tf_op jit(solution)/shard_map/pallas_call | solution.py:756
  36.5 0.0 copy-done
  36.5 0.0 copy-done.1
  36.5 0.0 copy-done.2
  36.5 3.1 %shard_map.114 = (f32[5,32,32,128]{3,2,1,0:T(8,128)}, f32[5,32,32,128]{3,2,1,0:T(8,128)}) custom-call(f32[32,32,128]{2,1,0:T(8,128)S(1)} %copy-done.1, f32[3,32,32,128]{3,2,1,0:T(8,128)S(1)} %copy-done, f32[32,32,128]{2,1,0:T(8,128)S(1)} %copy-done.2, f32[5,32,32,128]{3,2,1,0:T(8,128)S(1)} %get-tuple-element.6.part, ...), custom_call_target="tpu_custom_call" | custom-call | flops 10000000 | bytes 10000000 | tf_op jit(solution)/shard_map/pallas_call | solution.py:819
Async XLA Ops:
  0.6 35.9 %copy-start = (f32[3,32,32,128]{3,2,1,0:T(8,128)S(1)}, f32[3,32,32,128]{3,2,1,0:T(8,128)}, u32[]{:S(2)}) copy-start(f32[3,32,32,128]{3,2,1,0:T(8,128)} %mom.1) | copy-start | bytes 4718596
  0.6 35.9 %copy-start.1 = (f32[32,32,128]{2,1,0:T(8,128)S(1)}, f32[32,32,128]{2,1,0:T(8,128)}, u32[]{:S(2)}) copy-start(f32[32,32,128]{2,1,0:T(8,128)} %den.1) | copy-start | bytes 1572868
  0.7 35.9 %copy-start.2 = (f32[32,32,128]{2,1,0:T(8,128)S(1)}, f32[32,32,128]{2,1,0:T(8,128)}, u32[]{:S(2)}) copy-start(f32[32,32,128]{2,1,0:T(8,128)} %ene.1) | copy-start | bytes 1572868

commit v3 on v2

--- a/solution.py
+++ b/solution.py
@@ -255,6 +255,7 @@
     fy,
     fz,
     uv0,
+    moments_x,
     sy,
     sz,
     dys,
@@ -285,7 +286,7 @@
     rows = size_y // nx
     ratio, amplitude, corner = compact_kernel()
     filter_ratio, _ = decay(filter_alpha)
-    gain_d, near_d, far_d, corner_d, first_d = filtered_derivative()
+    gain_d, _, far_d, corner_d, first_d = filtered_derivative()
     half_rows = fields * rows
     farthest = sorted(range(1, nx), key=lambda k: -min(k, nx - k))
 
@@ -347,7 +348,7 @@
             acc = list(acc)
             for inner in range(unroll):
                 x = step * unroll + inner
-                w = [wtab[k, x] for k in range(2)]
+                w = [wtab[k, x] for k in range(4)]
                 rho, energy = den[x, ys, :], ene[x, ys, :]
                 m = [mom[j, x, ys, :] for j in range(3)]
                 inverse = 1.0 / rho
@@ -359,17 +360,63 @@
                 flux_x = (m[0], own[0] + pressure, m12, m13, total * v[0])
                 flux_y = (m[1], m12, own[1] + pressure, m23, total * v[1])
                 flux_z = (m[2], m13, m23, own[2] + pressure, total * v[2])
+                state = (rho, m[0], m[1], m[2], energy)
                 for f in range(fields):
                     fx[f, x, ys, :] = flux_x[f]
                     fy[f, x, ys, :] = flux_y[f]
                     fz[f, x, ys, :] = flux_z[f]
-                    acc[f] = acc[f] + w[0] * flux_y[f]
-                    acc[5 + f] = acc[5 + f] + w[1] * flux_y[f]
-                    acc[10 + f] = acc[10 + f] + w[0] * flux_z[f]
-                    acc[15 + f] = acc[15 + f] + w[1] * flux_z[f]
+                    change = (time_step * gain_d) * flux_x[f]
+                    acc[f] = acc[f] + w[0] * (state[f] - change)
+                    acc[5 + f] = acc[5 + f] + w[1] * (state[f] + change)
+                    acc[10 + f] = acc[10 + f] + w[2] * flux_x[f]
+                    acc[15 + f] = acc[15 + f] + w[3] * flux_x[f]
             return tuple(acc)
 
         acc = lax.fori_loop(0, size_x // unroll, cells, (zero,) * 20)
+        for f in range(fields):
+            uv0[0, f, ys, :] = acc[f]
+            uv0[1, f, ys, :] = acc[5 + f]
+            moments_x[0, f, ys, :] = acc[10 + f]
+            moments_x[1, f, ys, :] = acc[15 + f]
+            xn_out[0, f, ys, :] = fx[f, size_x - 1, ys, :]
+            xn_out[1, f, ys, :] = fx[f, 0, ys, :]
+        return 0
+
+    sy[10:16] = jnp.zeros((6, size_y, size_z), jnp.float32)
+    sz[:, 5:8] = jnp.zeros((2, 3, size_y, size_z), jnp.float32)
+    lax.fori_loop(0, size_y // 8, flux_chunk, 0)
+
+    def deal(message, side, f, values):
+        for owner in range(nx):
+            place = side * half_rows + rows * f
+            message[owner, place : place + rows, :] = values[rows * owner : rows * owner + rows]
+
+    pl.semaphore_wait(barrier, nx + ny + nz - 3)
+    for side in range(2):
+        for f in range(fields):
+            deal(xm_out, side, f, moments_x[side, f])
+    xm = [remote(xm_out.at[along("gx", k)], xm_in.at[k], "gx", k) for k in farthest]
+    for copy in xm:
+        copy.start()
+    xm_in[0] = xm_out[me_x]
+
+    def sums_chunk(chunk, _):
+        ys = pl.ds(pl.multiple_of(chunk * 8, 8), 8)
+
+        def sums(step, acc):
+            acc = list(acc)
+            for inner in range(unroll):
+                x = step * unroll + inner
+                w = [wtab[k, x] for k in range(2)]
+                for f in range(fields):
+                    value_y, value_z = fy[f, x, ys, :], fz[f, x, ys, :]
+                    acc[f] = acc[f] + w[0] * value_y
+                    acc[5 + f] = acc[5 + f] + w[1] * value_y
+                    acc[10 + f] = acc[10 + f] + w[0] * value_z
+                    acc[15 + f] = acc[15 + f] + w[1] * value_z
+            return tuple(acc)
+
+        acc = lax.fori_loop(0, size_x // unroll, sums, (zero,) * 20)
         for f in range(fields):
             sy[f, ys, :] = acc[f]
             sy[5 + f, ys, :] = acc[5 + f]
@@ -377,9 +424,7 @@
             sz[1, f, ys, :] = acc[15 + f]
         return 0
 
-    sy[10:16] = jnp.zeros((6, size_y, size_z), jnp.float32)
-    sz[:, 5:8] = jnp.zeros((2, 3, size_y, size_z), jnp.float32)
-    lax.fori_loop(0, size_y // 8, flux_chunk, 0)
+    lax.fori_loop(0, size_y // 8, sums_chunk, 0)
 
     for load in loads[1:]:
         load.wait()
@@ -425,8 +470,6 @@
     def span_carries(received):
         high, low = split(received)
         return product(jnp.concatenate([high, low, high], axis=0), pz[...], ((0,), (0,)))
-
-    pl.semaphore_wait(barrier, nx + ny + nz - 3)
 
     for group, (local, moments) in enumerate(apply_wall(sy[0:8], sy[8:16])):
         dys[8 * group : 8 * group + 8] = local
@@ -444,36 +487,6 @@
         copy.start()
     dzs[...] = span_local(sz[...].reshape(16 * size_y, size_z)).reshape(2, 8, size_y, size_z)
 
-    def stream_chunk(chunk, _):
-        ys = pl.ds(pl.multiple_of(chunk * 8, 8), 8)
-
-        def sums(step, acc):
-            acc = list(acc)
-            for inner in range(unroll):
-                x = step * unroll + inner
-                w = [wtab[k, x] for k in range(4)]
-                state = (den[x, ys, :], mom[0, x, ys, :], mom[1, x, ys, :], mom[2, x, ys, :], ene[x, ys, :])
-                for f in range(fields):
-                    flux = fx[f, x, ys, :]
-                    change = (time_step * gain_d) * flux
-                    acc[f] = acc[f] + w[0] * (state[f] - change)
-                    acc[5 + f] = acc[5 + f] + w[1] * (state[f] + change)
-                    acc[10 + f] = acc[10 + f] + w[2] * flux
-                    acc[15 + f] = acc[15 + f] + w[3] * flux
-            return tuple(acc)
-
-        acc = lax.fori_loop(0, size_x // unroll, sums, (zero,) * 20)
-        for f in range(fields):
-            uv0[0, f, ys, :] = acc[f]
-            uv0[1, f, ys, :] = acc[5 + f]
-            xn_out[0, 0, f, ys, :] = acc[10 + f]
-            xn_out[0, 1, f, ys, :] = fx[f, size_x - 1, ys, :]
-            xn_out[1, 0, f, ys, :] = acc[15 + f]
-            xn_out[1, 1, f, ys, :] = fx[f, 0, ys, :]
-        return 0
-
-    lax.fori_loop(0, size_y // 8, stream_chunk, 0)
-
     def wall_field(f, _):
         for part in range(size_x // 16):
             pair = [pl.ds(16 * part + 8 * side, 8) for side in range(2)]
@@ -494,11 +507,6 @@
     def span_carries(received):
         high, low = split(received)
         return product(jnp.concatenate([high, low, high], axis=0), pz[...], ((0,), (0,)))
-
-    def deal(message, side, f, values):
-        for owner in range(nx):
-            place = side * half_rows + rows * f
-            message[owner, place : place + rows, :] = values[rows * owner : rows * owner + rows]
 
     for copy in ys + zs:
         copy.wait()
@@ -522,13 +530,6 @@
     ]
     for copy in xn:
         copy.start()
-    for side in range(2):
-        for f in range(fields):
-            deal(xm_out, side, f, xn_out[side, 0, f])
-    xm = [remote(xm_out.at[along("gx", k)], xm_in.at[k], "gx", k) for k in farthest]
-    for copy in xm:
-        copy.start()
-    xm_in[0] = xm_out[me_x]
 
     half = size_x // 2
 
@@ -566,19 +567,22 @@
         return result
 
     from_behind = lax.broadcasted_iota(jnp.int32, (2 * half_rows, size_z), 0) < half_rows
-    for copy in xm:
-        copy.wait()
-    power = ratio**size_x
-    values = [xm_in[k] for k in range(nx)]
-    near_l, near_r = sweep(True, power, values), sweep(False, power, values)
-    for k in range(nx):
-        xo_out[k] = float(power) * jnp.where(from_behind, near_l[(k + 1) % nx], near_r[(k - 1) % nx])
-    xo = [remote(xo_out.at[k], xo_in.at[me_x], "gx", -k) for k in farthest]
-    for copy in xo:
-        copy.start()
-    xo_in[me_x] = xo_out[0]
-    for copy in xn:
-        copy.wait()
+    from_behind = lax.broadcasted_iota(jnp.int32, (2 * half_rows, size_z), 0) < half_rows
+
+    def solve_lines(arriving, received, power, answers, landing):
+        for copy in arriving:
+            copy.wait()
+        values = [received[k] for k in range(nx)]
+        behind, ahead = sweep(True, power, values), sweep(False, power, values)
+        for k in range(nx):
+            answers[k] = jnp.where(from_behind, behind[k], ahead[k])
+        leaving = [remote(answers.at[k], landing.at[me_x], "gx", -k) for k in farthest]
+        for copy in leaving:
+            copy.start()
+        landing[me_x] = answers[0]
+        return leaving
+
+    xo = solve_lines(xm, xm_in, ratio**size_x, xo_out, xo_in)
 
     def scan_chunk(chunk, _):
         ys = pl.ds(pl.multiple_of(chunk * 8, 8), 8)
@@ -597,34 +601,20 @@
             return tuple(carried)
 
         for side in range(2):
-            start = [xn_in[side, kind, f, ys, :] for kind in range(2) for f in range(fields)]
-            lax.fori_loop(0, size_x // unroll, functools.partial(scan, side), tuple(start))
+            lax.fori_loop(0, size_x // unroll, functools.partial(scan, side), (zero,) * 10)
         return 0
 
     lax.fori_loop(0, size_y // 8, scan_chunk, 0)
 
-    for copy in uv:
+    io = solve_lines(uv, uv_in, filter_ratio**size_x, io_out, io_in)
+    for copy in xn:
         copy.wait()
-    filter_power = filter_ratio**size_x
-    values = [uv_in[k] for k in range(nx)]
-    filter_l, filter_r = sweep(True, filter_power, values), sweep(False, filter_power, values)
-    for k in range(nx):
-        io_out[k] = jnp.where(from_behind, filter_l[k], filter_r[k])
-    io = [remote(io_out.at[k], io_in.at[me_x], "gx", -k) for k in farthest]
-    for copy in io:
-        copy.start()
-    io_in[me_x] = io_out[0]
+    tend[:, 0] += corner * xn_in[0]
+    tend[:, size_x - 1] -= corner * xn_in[1]
 
     for side in range(2):
         sign = -time_step if side else time_step
-        for f in range(fields):
-            past = xn_out[1 - side, 0, f] + float(power) * xn_in[1 - side, 0, f]
-            carry_d[side, f] = (
-                (sign * near_d) * xn_in[side, 0, f]
-                + (sign * corner_d) * xn_in[side, 1, f]
-                + (sign * far_d) * past
-                + (sign * first_d) * xn_out[1 - side, 1, f]
-            )
+        carry_d[side] = sign * (corner_d * xn_in[side] + far_d * moments_x[1 - side] + first_d * xn_out[1 - side])
 
     for copy in yb + zm:
         copy.wait()
@@ -682,22 +672,22 @@
         def state(f, x):
             return den[x, ys, :] if f == 0 else ene[x, ys, :] if f == 4 else mom[f - 1, x, ys, :]
 
-        far_l = [carried_in(carry_x, 0, f) for f in range(fields)]
-        far_r = [carried_in(carry_x, 1, f) for f in range(fields)]
+        from_l = [carried_in(carry_x, 0, f) for f in range(fields)]
+        from_r = [carried_in(carry_x, 1, f) for f in range(fields)]
         start_l = [
             carried_in(carry_f, 0, f)
             + carry_d[0, f, ys, :]
-            + time_step * (near_d * far_l[f] + float(far_d * power) * far_r[f])
+            + time_step * (near_d * from_l[f] + float(far_d * power) * from_r[f])
             for f in range(fields)
         ]
         start_r = [
             carried_in(carry_f, 1, f)
             + carry_d[1, f, ys, :]
-            - time_step * (near_d * far_r[f] + float(far_d * power) * far_l[f])
+            - time_step * (near_d * from_r[f] + float(far_d * power) * from_l[f])
             for f in range(fields)
         ]
-        head = [float(far_gain * ratio ** (size_x - 1)) * far_l[f] for f in range(fields)]
-        tail = [far_gain * far_r[f] for f in range(fields)]
+        head = [float(far_gain * ratio ** (size_x - 1)) * from_l[f] for f in range(fields)]
+        tail = [far_gain * from_r[f] for f in range(fields)]
 
         def back(step, carried):
             carried = list(carried)
@@ -781,6 +771,7 @@
                 pltpu.VMEM(cells, float32),
                 pltpu.VMEM(cells, float32),
                 pltpu.VMEM(sides, float32),
+                pltpu.VMEM(sides, float32),
                 pltpu.VMEM((16, size_y, size_z), float32),
                 pltpu.VMEM((2, 8, size_y, size_z), float32),
                 pltpu.VMEM((16, size_y, size_z), float32),
@@ -791,8 +782,8 @@
                 pltpu.VMEM((4, fields, size_x, size_z), float32),
                 pltpu.VMEM((8, fields, size_x, size_z), float32),
                 pltpu.VMEM((nz, fields, 8, size_x // 2 * size_y), float32),
-                pltpu.VMEM((2, 2, fields, size_y, size_z), float32),
-                pltpu.VMEM((2, 2, fields, size_y, size_z), float32),
+                pltpu.VMEM(sides, float32),
+                pltpu.VMEM(sides, float32),
                 pltpu.VMEM(owned, float32),
                 pltpu.VMEM(owned, float32),
                 pltpu.VMEM(owned, float32),

time: 39.8 us -> 34 us (0.85)
  Pallas kernels: 39 us -> 33.2 us
    pallas_call x1, Pallas kernels: 35.8 us -> 30.1 us  [on_device(): pl.pallas_call(functools.partial(exchange_kernel, nx, ny, nz), out_shape=...]
where the time goes in v3:
time: 34 us; the launch traced here: 33.9 us
  Pallas kernels  33.2 us (98%)
  between operations  0.69 us (2%)
    pallas_call x1, Pallas kernels, on_device(): pl.pallas_call(functools.partial(exchange_kernel, nx, ny, nz), out_shape=...  30.1 us
    pallas_call x1, Pallas kernels, on_device(): pl.pallas_call(filter_kernel, out_shape=[jax.ShapeDtypeStruct(cells, floa...  3.14 us

profile of v3, /device:TPU:1, one launch (start us, length us, event | category | flops | bytes accessed | tf_op | source)
XLA Modules:
  0.0 33.9 jit_solution(5888090814991374011)
XLA Ops:
  0.6 0.0 copy-start
  0.6 0.0 copy-start.1
  0.7 0.0 copy-start.2
  0.7 30.1 %shard_map.113 = (f32[5,32,32,128]{3,2,1,0:T(8,128)S(1)}, f32[16,20,128]{2,1,0:T(8,128)S(1)}, f32[16,20,128]{2,1,0:T(8,128)S(1)}, f32[2,5,32,128]{3,2,1,0:T(8,128)S(1)}) custom-call(f32[32,32,128]{2,1,0:T(8,128)} %den.1, f32[3,32,32,128]{3,2,1,0:T(8,128)} %mom.1, f32[32,32,128]{2,1,0:T(8,128)} %ene.1, f32[1,128]{1,0:T(1,128)} %bitcast.1, ...), custom_call_target="tpu_custom_call" | custom-call | flops 4000000000 | bytes 10000000 | tf_op jit(solution)/shard_map/pallas_call | solution.py:746
  30.8 0.0 copy-done
  30.8 0.0 copy-done.1
  30.8 0.0 copy-done.2
  30.8 3.1 %shard_map.114 = (f32[5,32,32,128]{3,2,1,0:T(8,128)}, f32[5,32,32,128]{3,2,1,0:T(8,128)}) custom-call(f32[32,32,128]{2,1,0:T(8,128)S(1)} %copy-done.1, f32[3,32,32,128]{3,2,1,0:T(8,128)S(1)} %copy-done, f32[32,32,128]{2,1,0:T(8,128)S(1)} %copy-done.2, f32[5,32,32,128]{3,2,1,0:T(8,128)S(1)} %get-tuple-element.6.part, ...), custom_call_target="tpu_custom_call" | custom-call | flops 10000000 | bytes 10000000 | tf_op jit(solution)/shard_map/pallas_call | solution.py:810
Async XLA Ops:
  0.6 30.1 %copy-start = (f32[3,32,32,128]{3,2,1,0:T(8,128)S(1)}, f32[3,32,32,128]{3,2,1,0:T(8,128)}, u32[]{:S(2)}) copy-start(f32[3,32,32,128]{3,2,1,0:T(8,128)} %mom.1) | copy-start | bytes 4718596
  0.6 30.1 %copy-start.1 = (f32[32,32,128]{2,1,0:T(8,128)S(1)}, f32[32,32,128]{2,1,0:T(8,128)}, u32[]{:S(2)}) copy-start(f32[32,32,128]{2,1,0:T(8,128)} %den.1) | copy-start | bytes 1572868
  0.7 30.1 %copy-start.2 = (f32[32,32,128]{2,1,0:T(8,128)S(1)}, f32[32,32,128]{2,1,0:T(8,128)}, u32[]{:S(2)}) copy-start(f32[32,32,128]{2,1,0:T(8,128)} %ene.1) | copy-start | bytes 1572868

commit v4 on v3

--- a/solution.py
+++ b/solution.py
@@ -238,6 +238,7 @@
     carry_x,
     carry_f,
     carry_d,
+    carry_n,
     den,
     mom,
     ene,
@@ -268,12 +269,14 @@
     zm_in,
     xn_out,
     xn_in,
+    pair_in,
     xm_out,
     xm_in,
     uv_out,
     uv_in,
     xo_out,
     xo_in,
+    xp_in,
     io_out,
     io_in,
     state_sem,
@@ -288,7 +291,13 @@
     filter_ratio, _ = decay(filter_alpha)
     gain_d, _, far_d, corner_d, first_d = filtered_derivative()
     half_rows = fields * rows
-    farthest = sorted(range(1, nx), key=lambda k: -min(k, nx - k))
+    chips = nx // 2
+    chip, core = me_x // 2, lax.rem(me_x, 2)
+    pair = 1 - 2 * core
+    half_y = size_y // 2
+
+    def farthest(count):
+        return sorted(range(1, count), key=lambda k: -min(k, count - k))
 
     def along(axis, offset):
         me, count = {"gx": (me_x, nx), "gy": (me_y, ny), "gz": (me_z, nz)}[axis]
@@ -314,6 +323,8 @@
             load.start()
     for load in loads[1:]:
         load.start()
+
+    yb_in[...] = jnp.zeros(yb_in.shape, jnp.float32)
 
     barrier = pltpu.get_barrier_semaphore()
     for axis, count in (("gx", nx), ("gy", ny), ("gz", nz)):
@@ -387,18 +398,13 @@
     lax.fori_loop(0, size_y // 8, flux_chunk, 0)
 
     def deal(message, side, f, values):
-        for owner in range(nx):
+        for owner in range(values.shape[0] // rows):
             place = side * half_rows + rows * f
             message[owner, place : place + rows, :] = values[rows * owner : rows * owner + rows]
 
     pl.semaphore_wait(barrier, nx + ny + nz - 3)
-    for side in range(2):
-        for f in range(fields):
-            deal(xm_out, side, f, moments_x[side, f])
-    xm = [remote(xm_out.at[along("gx", k)], xm_in.at[k], "gx", k) for k in farthest]
-    for copy in xm:
-        copy.start()
-    xm_in[0] = xm_out[me_x]
+    to_pair = remote(moments_x, pair_in, "gx", pair)
+    to_pair.start()
 
     def sums_chunk(chunk, _):
         ys = pl.ds(pl.multiple_of(chunk * 8, 8), 8)
@@ -487,6 +493,21 @@
         copy.start()
     dzs[...] = span_local(sz[...].reshape(16 * size_y, size_z)).reshape(2, 8, size_y, size_z)
 
+    to_pair.wait()
+    power = float(ratio**size_x)
+    second = core == 1
+    mine = pl.ds(pl.multiple_of(half_y * core, 8), half_y)
+    for side in range(2):
+        is_near = second if side == 0 else jnp.logical_not(second)
+        own_gain, pair_gain = jnp.where(is_near, 1.0, power), jnp.where(is_near, power, 1.0)
+        for f in range(fields):
+            deal(xm_out, side, f, own_gain * moments_x[side, f, mine, :] + pair_gain * pair_in[side, f, mine, :])
+        carry_n[side] = jnp.where(is_near, 1.0, 0.0) * pair_in[side]
+    xm = [remote(xm_out.at[lax.rem(chip + k, chips)], xm_in.at[k], "gx", 2 * k) for k in farthest(chips)]
+    for copy in xm:
+        copy.start()
+    xm_in[0] = xm_out[chip]
+
     def wall_field(f, _):
         for part in range(size_x // 16):
             pair = [pl.ds(16 * part + 8 * side, 8) for side in range(2)]
@@ -496,17 +517,17 @@
         return 0
 
     lax.fori_loop(0, fields, wall_field, 0)
-    yb = [
-        remote(yb_out.at[pl.ds(0, 3)], yb_in.at[pl.ds(0, 3)], "gy", 1),
-        remote(yb_out.at[pl.ds(1, 2)], yb_in.at[pl.ds(3, 2)], "gy", 2),
-        remote(yb_out.at[pl.ds(1, 3)], yb_in.at[pl.ds(5, 3)], "gy", 3),
-    ]
-    for copy in yb:
-        copy.start()
-
-    def span_carries(received):
-        high, low = split(received)
-        return product(jnp.concatenate([high, low, high], axis=0), pz[...], ((0,), (0,)))
+    yb = []
+    for distance in range(1, ny):
+        count = 2 if distance == 1 else 1
+        up_place = KINDS_Y.index((distance, "last" if distance == 1 else "ml"))
+        down_place = KINDS_Y.index((ny - distance, "mr"))
+        up = remote(yb_out.at[pl.ds(2 - count, count)], yb_in.at[pl.ds(up_place, count)], "gy", distance)
+        down = remote(yb_out.at[pl.ds(2, count)], yb_in.at[pl.ds(down_place, count)], "gy", -distance)
+        has_above, has_below = me_y < ny - distance, me_y >= distance
+        yb += [(up, has_above, has_below), (down, has_below, has_above)]
+    for copy, sends, _ in yb:
+        pl.when(sends)(copy.start)
 
     for copy in ys + zs:
         copy.wait()
@@ -519,7 +540,7 @@
             change = dys[unit] + wall[place : place + size_y, lane : lane + size_z]
             change = change + dzs[side, f] + span[f * size_y : (f + 1) * size_y, side * size_z : (side + 1) * size_z]
             deal(uv_out, side, f, uv0[side, f] - time_step * change)
-    uv = [remote(uv_out.at[along("gx", k)], uv_in.at[k], "gx", k) for k in farthest]
+    uv = [remote(uv_out.at[along("gx", k)], uv_in.at[k], "gx", k) for k in farthest(nx)]
     for copy in uv:
         copy.start()
     uv_in[0] = uv_out[me_x]
@@ -552,37 +573,52 @@
     lax.fori_loop(0, fields, span_cells, 0)
 
     def sweep(behind, power, values):
-        step = 1 if behind else -1
-        total = values[0] if behind else values[nx - 1]
-        for k in range(1, nx):
-            total = total + float(power**k) * (values[k] if behind else values[nx - 1 - k])
-        total = total * float(1.0 / (1.0 - power**nx))
-        place = nx - 1 if behind else 0
-        result = [None] * nx
+        step, count = 1 if behind else -1, len(values)
+        total = values[0] if behind else values[count - 1]
+        for k in range(1, count):
+            total = total + float(power**k) * (values[k] if behind else values[count - 1 - k])
+        total = total * float(1.0 / (1.0 - power**count))
+        place = count - 1 if behind else 0
+        result = [None] * count
         result[place] = total
-        for _ in range(nx - 1):
+        for _ in range(count - 1):
             total = values[place] + float(power) * total
             place = place - step
             result[place] = total
         return result
 
     from_behind = lax.broadcasted_iota(jnp.int32, (2 * half_rows, size_z), 0) < half_rows
-    from_behind = lax.broadcasted_iota(jnp.int32, (2 * half_rows, size_z), 0) < half_rows
-
-    def solve_lines(arriving, received, power, answers, landing):
-        for copy in arriving:
-            copy.wait()
-        values = [received[k] for k in range(nx)]
+
+    def solve_lines(received, power, answers):
+        values = [received[k] for k in range(received.shape[0])]
         behind, ahead = sweep(True, power, values), sweep(False, power, values)
-        for k in range(nx):
+        for k in range(len(values)):
             answers[k] = jnp.where(from_behind, behind[k], ahead[k])
-        leaving = [remote(answers.at[k], landing.at[me_x], "gx", -k) for k in farthest]
-        for copy in leaving:
-            copy.start()
-        landing[me_x] = answers[0]
-        return leaving
-
-    xo = solve_lines(xm, xm_in, ratio**size_x, xo_out, xo_in)
+
+    for copy in xm:
+        copy.wait()
+    solve_lines(xm_in, ratio ** (2 * size_x), xo_out)
+    xo = [remote(xo_out.at[k], xo_in.at[chip], "gx", -2 * k) for k in farthest(chips)]
+    for copy in xo:
+        copy.start()
+    xo_in[chip] = xo_out[0]
+
+    for copy in uv:
+        copy.wait()
+    solve_lines(uv_in, filter_ratio**size_x, io_out)
+    io = [remote(io_out.at[k], io_in.at[me_x], "gx", -k) for k in farthest(nx)]
+    for copy in io:
+        copy.start()
+    io_in[me_x] = io_out[0]
+
+    for copy in xn:
+        copy.wait()
+    tend[:, 0] += corner * xn_in[0]
+    tend[:, size_x - 1] -= corner * xn_in[1]
+
+    for side in range(2):
+        sign = -time_step if side else time_step
+        carry_d[side] = sign * (corner_d * xn_in[side] + far_d * moments_x[1 - side] + first_d * xn_out[1 - side])
 
     def scan_chunk(chunk, _):
         ys = pl.ds(pl.multiple_of(chunk * 8, 8), 8)
@@ -606,18 +642,16 @@
 
     lax.fori_loop(0, size_y // 8, scan_chunk, 0)
 
-    io = solve_lines(uv, uv_in, filter_ratio**size_x, io_out, io_in)
-    for copy in xn:
+    for copy in xo:
         copy.wait()
-    tend[:, 0] += corner * xn_in[0]
-    tend[:, size_x - 1] -= corner * xn_in[1]
-
-    for side in range(2):
-        sign = -time_step if side else time_step
-        carry_d[side] = sign * (corner_d * xn_in[side] + far_d * moments_x[1 - side] + first_d * xn_out[1 - side])
-
-    for copy in yb + zm:
+    halves = remote(xo_in, xp_in, "gx", pair)
+    halves.start()
+
+    for copy in zm:
         copy.wait()
+    for copy, sends, receives in yb:
+        pl.when(sends)(copy.wait_send)
+        pl.when(receives)(copy.wait_recv)
 
     def carries(f, _):
         both = span_carries(zm_in[:, f].reshape(8 * nz, half * size_y))
@@ -634,13 +668,16 @@
 
     lax.fori_loop(0, fields, carries, 0)
 
-    for copy in xo + io:
+    halves.wait()
+    gains = jnp.where(from_behind, jnp.where(second, power, 1.0), jnp.where(second, 1.0, power))
+    carry_x[pl.ds(chips * core, chips)] = xo_in[...] * gains
+    carry_x[pl.ds(chips * (1 - core), chips)] = xp_in[...] * gains
+    for copy in io:
         copy.wait()
-    carry_x[...] = xo_in[...]
     carry_f[...] = io_in[...]
 
 
-def filter_kernel(den, mom, ene, part, carry_x, carry_f, carry_d, tend_hbm, after_hbm, tend, after, sems):
+def filter_kernel(den, mom, ene, part, carry_x, carry_f, carry_d, carry_n, tend_hbm, after_hbm, tend, after, sems):
     chunks, fields, size_x = tend.shape[:3]
     half_rows = carry_x.shape[1] // 2
     rows = half_rows // fields
@@ -672,8 +709,8 @@
         def state(f, x):
             return den[x, ys, :] if f == 0 else ene[x, ys, :] if f == 4 else mom[f - 1, x, ys, :]
 
-        from_l = [carried_in(carry_x, 0, f) for f in range(fields)]
-        from_r = [carried_in(carry_x, 1, f) for f in range(fields)]
+        from_l = [carried_in(carry_x, 0, f) + carry_n[0, f, ys, :] for f in range(fields)]
+        from_r = [carried_in(carry_x, 1, f) + carry_n[1, f, ys, :] for f in range(fields)]
         start_l = [
             carried_in(carry_f, 0, f)
             + carry_d[0, f, ys, :]
@@ -738,21 +775,23 @@
         wtab = stream_weights(size_x).astype(np.float32)
         cells = (fields, size_x, size_y, size_z)
         owned = (nx, 2 * fields * rows, size_z)
+        chipwise = (nx // 2, 2 * fields * rows, size_z)
         sides = (2, fields, size_y, size_z)
         vmem = pl.BlockSpec(memory_space=pltpu.VMEM)
         stays = pl.BlockSpec(memory_space=pltpu.HBM)
-        copies = 2 + 4 * (nx - 1) + 6 + 2 * (nz - 1)
+        copies = 7 + 2 * (nx - 1) + 2 * (nx // 2 - 1) + 2 * (ny - 1) + 2 * (nz - 1)
         chunks = size_y // 8
-        part, carry_x, carry_f, carry_d = pl.pallas_call(
+        part, carry_x, carry_f, carry_d, carry_n = pl.pallas_call(
             functools.partial(exchange_kernel, nx, ny, nz),
             out_shape=[
                 jax.ShapeDtypeStruct(cells, float32),
                 jax.ShapeDtypeStruct(owned, float32),
                 jax.ShapeDtypeStruct(owned, float32),
                 jax.ShapeDtypeStruct(sides, float32),
+                jax.ShapeDtypeStruct(sides, float32),
             ],
             in_specs=[stays] * 10,
-            out_specs=[vmem] * 4,
+            out_specs=[vmem] * 5,
             scratch_shapes=[
                 pltpu.VMEM(cells[1:], float32),
                 pltpu.VMEM((3,) + cells[1:], float32),
@@ -784,12 +823,14 @@
                 pltpu.VMEM((nz, fields, 8, size_x // 2 * size_y), float32),
                 pltpu.VMEM(sides, float32),
                 pltpu.VMEM(sides, float32),
+                pltpu.VMEM(sides, float32),
+                pltpu.VMEM(chipwise, float32),
+                pltpu.VMEM(chipwise, float32),
                 pltpu.VMEM(owned, float32),
                 pltpu.VMEM(owned, float32),
-                pltpu.VMEM(owned, float32),
-                pltpu.VMEM(owned, float32),
-                pltpu.VMEM(owned, float32),
-                pltpu.VMEM(owned, float32),
+                pltpu.VMEM(chipwise, float32),
+                pltpu.VMEM(chipwise, float32),
+                pltpu.VMEM(chipwise, float32),
                 pltpu.VMEM(owned, float32),
                 pltpu.VMEM(owned, float32),
                 pltpu.SemaphoreType.DMA((3, chunks)),
@@ -810,7 +851,7 @@
         return pl.pallas_call(
             filter_kernel,
             out_shape=[jax.ShapeDtypeStruct(cells, float32), jax.ShapeDtypeStruct(cells, float32)],
-            in_specs=[vmem] * 7,
+            in_specs=[vmem] * 8,
             out_specs=[stays] * 2,
             scratch_shapes=[
                 pltpu.VMEM((chunks, fields, size_x, 8, size_z), float32),
@@ -819,7 +860,7 @@
             ],
             compiler_params=pltpu.CompilerParams(vmem_limit_bytes=16 * 1024 * 1024),
             cost_estimate=pl.CostEstimate(flops=10**7, bytes_accessed=10**7, transcendentals=0),
-        )(density, momentum, energy, part, carry_x, carry_f, carry_d)
+        )(density, momentum, energy, part, carry_x, carry_f, carry_d, carry_n)
 
     return jax.shard_map(
         on_device,

time: 34 us -> 32.2 us (0.947)
  Pallas kernels: 33.2 us -> 31.4 us
    pallas_call x1, Pallas kernels: 30.1 us -> 28.2 us  [on_device(): pl.pallas_call(functools.partial(exchange_kernel, nx, ny, nz), out_shape=...]
where the time goes in v4:
time: 32.2 us; the launch traced here: 32.1 us
  Pallas kernels  31.4 us (98%)
  between operations  0.69 us (2%)
    pallas_call x1, Pallas kernels, on_device(): pl.pallas_call(functools.partial(exchange_kernel, nx, ny, nz), out_shape=...  28.2 us
    pallas_call x1, Pallas kernels, on_device(): pl.pallas_call(filter_kernel, out_shape=[jax.ShapeDtypeStruct(cells, floa...  3.16 us

profile of v4, /device:TPU:1, one launch (start us, length us, event | category | flops | bytes accessed | tf_op | source)
XLA Modules:
  0.0 32.1 jit_solution(9295727159959190385)
XLA Ops:
  0.6 0.0 copy-start
  0.6 0.0 copy-start.1
  0.7 0.0 copy-start.2
  0.7 28.2 %shard_map.113 = (f32[5,32,32,128]{3,2,1,0:T(8,128)S(1)}, f32[16,20,128]{2,1,0:T(8,128)S(1)}, f32[16,20,128]{2,1,0:T(8,128)S(1)}, f32[2,5,32,128]{3,2,1,0:T(8,128)S(1)}, f32[2,5,32,128]{3,2,1,0:T(8,128)S(1)}) custom-call(f32[32,32,128]{2,1,0:T(8,128)} %den.1, f32[3,32,32,128]{3,2,1,0:T(8,128)} %mom.1, f32[32,32,128]{2,1,0:T(8,128)} %ene.1, ...), custom_call_target="tpu_custom_call" | custom-call | flops 4000000000 | bytes 10000000 | tf_op jit(solution)/shard_map/pallas_call | solution.py:784
  28.9 0.0 copy-done
  28.9 0.0 copy-done.1
  28.9 0.0 copy-done.2
  28.9 3.2 %shard_map.114 = (f32[5,32,32,128]{3,2,1,0:T(8,128)}, f32[5,32,32,128]{3,2,1,0:T(8,128)}) custom-call(f32[32,32,128]{2,1,0:T(8,128)S(1)} %copy-done.1, f32[3,32,32,128]{3,2,1,0:T(8,128)S(1)} %copy-done, f32[32,32,128]{2,1,0:T(8,128)S(1)} %copy-done.2, f32[5,32,32,128]{3,2,1,0:T(8,128)S(1)} %get-tuple-element.7.part, ...), custom_call_target="tpu_custom_call" | custom-call | flops 10000000 | bytes 10000000 | tf_op jit(solution)/shard_map/pallas_call | solution.py:851
Async XLA Ops:
  0.6 28.3 %copy-start = (f32[3,32,32,128]{3,2,1,0:T(8,128)S(1)}, f32[3,32,32,128]{3,2,1,0:T(8,128)}, u32[]{:S(2)}) copy-start(f32[3,32,32,128]{3,2,1,0:T(8,128)} %mom.1) | copy-start | bytes 4718596
  0.6 28.3 %copy-start.1 = (f32[32,32,128]{2,1,0:T(8,128)S(1)}, f32[32,32,128]{2,1,0:T(8,128)}, u32[]{:S(2)}) copy-start(f32[32,32,128]{2,1,0:T(8,128)} %den.1) | copy-start | bytes 1572868
  0.7 28.3 %copy-start.2 = (f32[32,32,128]{2,1,0:T(8,128)S(1)}, f32[32,32,128]{2,1,0:T(8,128)}, u32[]{:S(2)}) copy-start(f32[32,32,128]{2,1,0:T(8,128)} %ene.1) | copy-start | bytes 1572868

commit v5 on v4

--- a/solution.py
+++ b/solution.py
@@ -303,6 +303,18 @@
         me, count = {"gx": (me_x, nx), "gy": (me_y, ny), "gz": (me_z, nz)}[axis]
         return lax.rem(me + offset + count, count)
 
+    class Group:
+        def __init__(self, copies, sent, received):
+            self.copies, self.sent, self.received = copies, sent, received
+
+        def start(self):
+            for copy in self.copies:
+                copy.start()
+
+        def wait(self):
+            for region, sem in (self.sent, self.received):
+                pltpu.make_async_copy(region, region, sem).wait()
+
     def state_loads(chunk):
         ys = pl.ds(pl.multiple_of(chunk * 8, 8), 8)
         return [
@@ -343,6 +355,25 @@
             recv_sem=recv_sem.at[place],
             device_id={axis: along(axis, offset)},
             device_id_type=MESH,
+        )
+
+    def remote_group(blocks, step, source, target):
+        place = next_sem[0]
+        next_sem[0] = place + 1
+        sems = send_sem.at[place], recv_sem.at[place]
+        copies = [
+            pltpu.make_async_remote_copy(
+                src_ref=source(k),
+                dst_ref=target(k),
+                send_sem=sems[0],
+                recv_sem=sems[1],
+                device_id={"gx": along("gx", step * k)},
+                device_id_type=MESH,
+            )
+            for k in farthest(blocks)
+        ]
+        return lambda out, arrived: Group(
+            copies, (out.at[pl.ds(0, blocks - 1)], sems[0]), (arrived.at[pl.ds(0, blocks - 1)], sems[1])
         )
 
     loads[0].wait()
@@ -503,9 +534,8 @@
         for f in range(fields):
             deal(xm_out, side, f, own_gain * moments_x[side, f, mine, :] + pair_gain * pair_in[side, f, mine, :])
         carry_n[side] = jnp.where(is_near, 1.0, 0.0) * pair_in[side]
-    xm = [remote(xm_out.at[lax.rem(chip + k, chips)], xm_in.at[k], "gx", 2 * k) for k in farthest(chips)]
-    for copy in xm:
-        copy.start()
+    xm = remote_group(chips, 2, lambda k: xm_out.at[lax.rem(chip + k, chips)], lambda k: xm_in.at[k])(xm_out, xm_in)
+    xm.start()
     xm_in[0] = xm_out[chip]
 
     def wall_field(f, _):
@@ -540,9 +570,8 @@
             change = dys[unit] + wall[place : place + size_y, lane : lane + size_z]
             change = change + dzs[side, f] + span[f * size_y : (f + 1) * size_y, side * size_z : (side + 1) * size_z]
             deal(uv_out, side, f, uv0[side, f] - time_step * change)
-    uv = [remote(uv_out.at[along("gx", k)], uv_in.at[k], "gx", k) for k in farthest(nx)]
-    for copy in uv:
-        copy.start()
+    uv = remote_group(nx, 1, lambda k: uv_out.at[along("gx", k)], lambda k: uv_in.at[k])(uv_out, uv_in)
+    uv.start()
     uv_in[0] = uv_out[me_x]
 
     xn = [
@@ -595,20 +624,16 @@
         for k in range(len(values)):
             answers[k] = jnp.where(from_behind, behind[k], ahead[k])
 
-    for copy in xm:
-        copy.wait()
+    xm.wait()
     solve_lines(xm_in, ratio ** (2 * size_x), xo_out)
-    xo = [remote(xo_out.at[k], xo_in.at[chip], "gx", -2 * k) for k in farthest(chips)]
-    for copy in xo:
-        copy.start()
+    xo = remote_group(chips, -2, lambda k: xo_out.at[k], lambda k: xo_in.at[chip])(xo_out, xo_in)
+    xo.start()
     xo_in[chip] = xo_out[0]
 
-    for copy in uv:
-        copy.wait()
+    uv.wait()
     solve_lines(uv_in, filter_ratio**size_x, io_out)
-    io = [remote(io_out.at[k], io_in.at[me_x], "gx", -k) for k in farthest(nx)]
-    for copy in io:
-        copy.start()
+    io = remote_group(nx, -1, lambda k: io_out.at[k], lambda k: io_in.at[me_x])(io_out, io_in)
+    io.start()
     io_in[me_x] = io_out[0]
 
     for copy in xn:
@@ -642,8 +667,7 @@
 
     lax.fori_loop(0, size_y // 8, scan_chunk, 0)
 
-    for copy in xo:
-        copy.wait()
+    xo.wait()
     halves = remote(xo_in, xp_in, "gx", pair)
     halves.start()
 
@@ -672,8 +696,7 @@
     gains = jnp.where(from_behind, jnp.where(second, power, 1.0), jnp.where(second, 1.0, power))
     carry_x[pl.ds(chips * core, chips)] = xo_in[...] * gains
     carry_x[pl.ds(chips * (1 - core), chips)] = xp_in[...] * gains
-    for copy in io:
-        copy.wait()
+    io.wait()
     carry_f[...] = io_in[...]
 
 
@@ -779,7 +802,7 @@
         sides = (2, fields, size_y, size_z)
         vmem = pl.BlockSpec(memory_space=pltpu.VMEM)
         stays = pl.BlockSpec(memory_space=pltpu.HBM)
-        copies = 7 + 2 * (nx - 1) + 2 * (nx // 2 - 1) + 2 * (ny - 1) + 2 * (nz - 1)
+        copies = 11 + 2 * (ny - 1) + 2 * (nz - 1)
         chunks = size_y // 8
         part, carry_x, carry_f, carry_d, carry_n = pl.pallas_call(
             functools.partial(exchange_kernel, nx, ny, nz),

time: 32.2 us -> 31.5 us (0.978)
  Pallas kernels: 31.4 us -> 30.7 us
    pallas_call x1, Pallas kernels: 28.2 us -> 27.5 us  [on_device(): pl.pallas_call(functools.partial(exchange_kernel, nx, ny, nz), out_shape=...]
where the time goes in v5:
time: 31.5 us; the launch traced here: 31.4 us
  Pallas kernels  30.7 us (97%)
  between operations  0.69 us (2%)
    pallas_call x1, Pallas kernels, on_device(): pl.pallas_call(functools.partial(exchange_kernel, nx, ny, nz), out_shape=...  27.5 us
    pallas_call x1, Pallas kernels, on_device(): pl.pallas_call(filter_kernel, out_shape=[jax.ShapeDtypeStruct(cells, floa...  3.16 us

profile of v5, /device:TPU:1, one launch (start us, length us, event | category | flops | bytes accessed | tf_op | source)
XLA Modules:
  0.0 31.4 jit_solution(10739831405837090686)
XLA Ops:
  0.6 0.0 copy-start
  0.6 0.0 copy-start.1
  0.7 0.0 copy-start.2
  0.7 27.5 %shard_map.113 = (f32[5,32,32,128]{3,2,1,0:T(8,128)S(1)}, f32[16,20,128]{2,1,0:T(8,128)S(1)}, f32[16,20,128]{2,1,0:T(8,128)S(1)}, f32[2,5,32,128]{3,2,1,0:T(8,128)S(1)}, f32[2,5,32,128]{3,2,1,0:T(8,128)S(1)}) custom-call(f32[32,32,128]{2,1,0:T(8,128)} %den.1, f32[3,32,32,128]{3,2,1,0:T(8,128)} %mom.1, f32[32,32,128]{2,1,0:T(8,128)} %ene.1, ...), custom_call_target="tpu_custom_call" | custom-call | flops 4000000000 | bytes 10000000 | tf_op jit(solution)/shard_map/pallas_call | solution.py:807
  28.2 0.0 copy-done
  28.2 0.0 copy-done.1
  28.2 0.0 copy-done.2
  28.2 3.2 %shard_map.114 = (f32[5,32,32,128]{3,2,1,0:T(8,128)}, f32[5,32,32,128]{3,2,1,0:T(8,128)}) custom-call(f32[32,32,128]{2,1,0:T(8,128)S(1)} %copy-done.1, f32[3,32,32,128]{3,2,1,0:T(8,128)S(1)} %copy-done, f32[32,32,128]{2,1,0:T(8,128)S(1)} %copy-done.2, f32[5,32,32,128]{3,2,1,0:T(8,128)S(1)} %get-tuple-element.7.part, ...), custom_call_target="tpu_custom_call" | custom-call | flops 10000000 | bytes 10000000 | tf_op jit(solution)/shard_map/pallas_call | solution.py:874
Async XLA Ops:
  0.6 27.6 %copy-start = (f32[3,32,32,128]{3,2,1,0:T(8,128)S(1)}, f32[3,32,32,128]{3,2,1,0:T(8,128)}, u32[]{:S(2)}) copy-start(f32[3,32,32,128]{3,2,1,0:T(8,128)} %mom.1) | copy-start | bytes 4718596
  0.6 27.6 %copy-start.1 = (f32[32,32,128]{2,1,0:T(8,128)S(1)}, f32[32,32,128]{2,1,0:T(8,128)}, u32[]{:S(2)}) copy-start(f32[32,32,128]{2,1,0:T(8,128)} %den.1) | copy-start | bytes 1572868
  0.7 27.6 %copy-start.2 = (f32[32,32,128]{2,1,0:T(8,128)S(1)}, f32[32,32,128]{2,1,0:T(8,128)}, u32[]{:S(2)}) copy-start(f32[32,32,128]{2,1,0:T(8,128)} %ene.1) | copy-start | bytes 1572868

commit v6 on v5

--- a/solution.py
+++ b/solution.py
@@ -312,8 +312,10 @@
                 copy.start()
 
         def wait(self):
-            for region, sem in (self.sent, self.received):
-                pltpu.make_async_copy(region, region, sem).wait()
+            pltpu.make_async_copy(self.received[0], self.received[0], self.received[1]).wait()
+
+        def wait_sent(self):
+            pltpu.make_async_copy(self.sent[0], self.sent[0], self.sent[1]).wait()
 
     def state_loads(chunk):
         ys = pl.ds(pl.multiple_of(chunk * 8, 8), 8)
@@ -630,21 +632,6 @@
     xo.start()
     xo_in[chip] = xo_out[0]
 
-    uv.wait()
-    solve_lines(uv_in, filter_ratio**size_x, io_out)
-    io = remote_group(nx, -1, lambda k: io_out.at[k], lambda k: io_in.at[me_x])(io_out, io_in)
-    io.start()
-    io_in[me_x] = io_out[0]
-
-    for copy in xn:
-        copy.wait()
-    tend[:, 0] += corner * xn_in[0]
-    tend[:, size_x - 1] -= corner * xn_in[1]
-
-    for side in range(2):
-        sign = -time_step if side else time_step
-        carry_d[side] = sign * (corner_d * xn_in[side] + far_d * moments_x[1 - side] + first_d * xn_out[1 - side])
-
     def scan_chunk(chunk, _):
         ys = pl.ds(pl.multiple_of(chunk * 8, 8), 8)
 
@@ -667,6 +654,21 @@
 
     lax.fori_loop(0, size_y // 8, scan_chunk, 0)
 
+    uv.wait()
+    solve_lines(uv_in, filter_ratio**size_x, io_out)
+    io = remote_group(nx, -1, lambda k: io_out.at[k], lambda k: io_in.at[me_x])(io_out, io_in)
+    io.start()
+    io_in[me_x] = io_out[0]
+
+    for copy in xn:
+        copy.wait()
+    tend[:, 0] += corner * xn_in[0]
+    tend[:, size_x - 1] -= corner * xn_in[1]
+
+    for side in range(2):
+        sign = -time_step if side else time_step
+        carry_d[side] = sign * (corner_d * xn_in[side] + far_d * moments_x[1 - side] + first_d * xn_out[1 - side])
+
     xo.wait()
     halves = remote(xo_in, xp_in, "gx", pair)
     halves.start()
@@ -692,6 +694,8 @@
 
     lax.fori_loop(0, fields, carries, 0)
 
+    for group in (xm, uv, xo, io):
+        group.wait_sent()
     halves.wait()
     gains = jnp.where(from_behind, jnp.where(second, power, 1.0), jnp.where(second, 1.0, power))
     carry_x[pl.ds(chips * core, chips)] = xo_in[...] * gains

time: 31.5 us -> 31.5 us (level)
  no operation moved by 1% of the time
where the time goes in v6:
time: 31.5 us; the launch traced here: 31.4 us
  Pallas kernels  30.7 us (97%)
  between operations  0.69 us (2%)
    pallas_call x1, Pallas kernels, on_device(): pl.pallas_call(functools.partial(exchange_kernel, nx, ny, nz), out_shape=...  27.6 us
    pallas_call x1, Pallas kernels, on_device(): pl.pallas_call(filter_kernel, out_shape=[jax.ShapeDtypeStruct(cells, floa...  3.16 us

profile of v6, /device:TPU:1, one launch (start us, length us, event | category | flops | bytes accessed | tf_op | source)
XLA Modules:
  0.0 31.4 jit_solution(8163003491632960570)
XLA Ops:
  0.6 0.0 copy-start
  0.6 0.0 copy-start.1
  0.7 0.0 copy-start.2
  0.7 27.6 %shard_map.113 = (f32[5,32,32,128]{3,2,1,0:T(8,128)S(1)}, f32[16,20,128]{2,1,0:T(8,128)S(1)}, f32[16,20,128]{2,1,0:T(8,128)S(1)}, f32[2,5,32,128]{3,2,1,0:T(8,128)S(1)}, f32[2,5,32,128]{3,2,1,0:T(8,128)S(1)}) custom-call(f32[32,32,128]{2,1,0:T(8,128)} %den.1, f32[3,32,32,128]{3,2,1,0:T(8,128)} %mom.1, f32[32,32,128]{2,1,0:T(8,128)} %ene.1, ...), custom_call_target="tpu_custom_call" | custom-call | flops 4000000000 | bytes 10000000 | tf_op jit(solution)/shard_map/pallas_call | solution.py:811
  28.3 0.0 copy-done
  28.3 0.0 copy-done.1
  28.3 0.0 copy-done.2
  28.3 3.2 %shard_map.114 = (f32[5,32,32,128]{3,2,1,0:T(8,128)}, f32[5,32,32,128]{3,2,1,0:T(8,128)}) custom-call(f32[32,32,128]{2,1,0:T(8,128)S(1)} %copy-done.1, f32[3,32,32,128]{3,2,1,0:T(8,128)S(1)} %copy-done, f32[32,32,128]{2,1,0:T(8,128)S(1)} %copy-done.2, f32[5,32,32,128]{3,2,1,0:T(8,128)S(1)} %get-tuple-element.7.part, ...), custom_call_target="tpu_custom_call" | custom-call | flops 10000000 | bytes 10000000 | tf_op jit(solution)/shard_map/pallas_call | solution.py:878
Async XLA Ops:
  0.6 27.6 %copy-start = (f32[3,32,32,128]{3,2,1,0:T(8,128)S(1)}, f32[3,32,32,128]{3,2,1,0:T(8,128)}, u32[]{:S(2)}) copy-start(f32[3,32,32,128]{3,2,1,0:T(8,128)} %mom.1) | copy-start | bytes 4718596
  0.6 27.6 %copy-start.1 = (f32[32,32,128]{2,1,0:T(8,128)S(1)}, f32[32,32,128]{2,1,0:T(8,128)}, u32[]{:S(2)}) copy-start(f32[32,32,128]{2,1,0:T(8,128)} %den.1) | copy-start | bytes 1572868
  0.7 27.6 %copy-start.2 = (f32[32,32,128]{2,1,0:T(8,128)S(1)}, f32[32,32,128]{2,1,0:T(8,128)}, u32[]{:S(2)}) copy-start(f32[32,32,128]{2,1,0:T(8,128)} %ene.1) | copy-start | bytes 1572868

commit v7 on v6

--- a/solution.py
+++ b/solution.py
@@ -380,7 +380,7 @@
 
     loads[0].wait()
 
-    unroll = 4
+    unroll = 8
     zero = jnp.zeros((8, size_z), jnp.float32)
 
     def flux_chunk(chunk, _):
@@ -715,7 +715,7 @@
     amplitude = (0.5 + filter_alpha - straight) * gain
     _, near_d, far_d, _, _ = filtered_derivative()
     power = ratio**size_x
-    unroll = 4
+    unroll = 8
 
     def copies(chunk):
         ys = pl.ds(pl.multiple_of(chunk * 8, 8), 8)

time: 31.5 us -> 31.2 us (level)
  no operation moved by 1% of the time
where the time goes in v7:
time: 31.2 us; the launch traced here: 31.1 us
  Pallas kernels  30.4 us (97%)
  between operations  0.69 us (2%)
    pallas_call x1, Pallas kernels, on_device(): pl.pallas_call(functools.partial(exchange_kernel, nx, ny, nz), out_shape=...  27.3 us
    pallas_call x1, Pallas kernels, on_device(): pl.pallas_call(filter_kernel, out_shape=[jax.ShapeDtypeStruct(cells, floa...  3.07 us

profile of v7, /device:TPU:1, one launch (start us, length us, event | category | flops | bytes accessed | tf_op | source)
XLA Modules:
  0.0 31.1 jit_solution(17401906005946660438)
XLA Ops:
  0.6 0.0 copy-start
  0.6 0.0 copy-start.1
  0.7 0.0 copy-start.2
  0.7 27.3 %shard_map.113 = (f32[5,32,32,128]{3,2,1,0:T(8,128)S(1)}, f32[16,20,128]{2,1,0:T(8,128)S(1)}, f32[16,20,128]{2,1,0:T(8,128)S(1)}, f32[2,5,32,128]{3,2,1,0:T(8,128)S(1)}, f32[2,5,32,128]{3,2,1,0:T(8,128)S(1)}) custom-call(f32[32,32,128]{2,1,0:T(8,128)} %den.1, f32[3,32,32,128]{3,2,1,0:T(8,128)} %mom.1, f32[32,32,128]{2,1,0:T(8,128)} %ene.1, ...), custom_call_target="tpu_custom_call" | custom-call | flops 4000000000 | bytes 10000000 | tf_op jit(solution)/shard_map/pallas_call | solution.py:811
  28.0 0.0 copy-done
  28.0 0.0 copy-done.1
  28.0 0.0 copy-done.2
  28.0 3.1 %shard_map.114 = (f32[5,32,32,128]{3,2,1,0:T(8,128)}, f32[5,32,32,128]{3,2,1,0:T(8,128)}) custom-call(f32[32,32,128]{2,1,0:T(8,128)S(1)} %copy-done.1, f32[3,32,32,128]{3,2,1,0:T(8,128)S(1)} %copy-done, f32[32,32,128]{2,1,0:T(8,128)S(1)} %copy-done.2, f32[5,32,32,128]{3,2,1,0:T(8,128)S(1)} %get-tuple-element.7.part, ...), custom_call_target="tpu_custom_call" | custom-call | flops 10000000 | bytes 10000000 | tf_op jit(solution)/shard_map/pallas_call | solution.py:878
Async XLA Ops:
  0.6 27.4 %copy-start = (f32[3,32,32,128]{3,2,1,0:T(8,128)S(1)}, f32[3,32,32,128]{3,2,1,0:T(8,128)}, u32[]{:S(2)}) copy-start(f32[3,32,32,128]{3,2,1,0:T(8,128)} %mom.1) | copy-start | bytes 4718596
  0.6 27.4 %copy-start.1 = (f32[32,32,128]{2,1,0:T(8,128)S(1)}, f32[32,32,128]{2,1,0:T(8,128)}, u32[]{:S(2)}) copy-start(f32[32,32,128]{2,1,0:T(8,128)} %den.1) | copy-start | bytes 1572868
  0.7 27.4 %copy-start.2 = (f32[32,32,128]{2,1,0:T(8,128)S(1)}, f32[32,32,128]{2,1,0:T(8,128)}, u32[]{:S(2)}) copy-start(f32[32,32,128]{2,1,0:T(8,128)} %ene.1) | copy-start | bytes 1572868
